TPU v7x, 512 devices: a whole 4x8x8 slice. The times are simulated.
512 devices in a mesh: grp: 16 (over z, core), tr: 32 (over x, y).
Axes of the slice: x: 4, y: 8, z: 8, core: 2. Of those that a mesh axis runs over, the one named last changes fastest.
Arguments:
- amplitudes: bfloat16 [512, 1, 32768], P('tr', None, 'grp'), may hold values from -6 to 6
- integrals: bfloat16 [1, 32768, 28672], P(None, 'grp', 'tr'), may hold values from -0.046875 to 0.046875
- slab_count: int32 [1, 16], P(None, 'grp'), may hold values from 512 to 2048, as said below
Outputs:
- ladder: bfloat16 [512, 1, 28672], P('grp', None, 'tr')
Inputs may be any that keep to these rules, and one draw needn't show every extreme that they name: `slab_count`: in every irrep block some slab holds exactly 2048 valid pairs.
All inputs are finite; a program needn't handle non-finite values.
Results may differ from a plain program's by a relative error of at most 0.001.
Values may be sent and summed in bfloat16 or wider, within the bound.
No kernel may reach another device: no remote copies, remote signals or barrier semaphores. Data moves between devices by JAX's collectives and lax.ppermute only.
A program may use at most 64 MiB of HBM per device.

v0:
```python
import jax
import jax.numpy as jnp
from jax import lax
from jax.sharding import PartitionSpec as P


def contract(rows, integrals):
    return jnp.einsum("inc,nca->ina", rows, integrals, preferred_element_type=jnp.float32)


def on_device(amplitudes, integrals, slab_count):
    width = amplitudes.shape[2]
    column = lax.broadcasted_iota(jnp.int32, (amplitudes.shape[1], width), 1)
    valid = column < slab_count
    masked = jnp.where(valid[None, :, :], amplitudes, jnp.zeros_like(amplitudes))
    whole = lax.all_gather(masked, "tr", axis=0, tiled=True)
    summed = lax.psum_scatter(contract(whole, integrals), "grp", scatter_dimension=0, tiled=True)
    return summed.astype(jnp.bfloat16)


def solution(mesh):
    return jax.shard_map(
        on_device,
        mesh=mesh,
        in_specs=(P("tr", None, "grp"), P(None, "grp", "tr"), P(None, "grp")),
        out_specs=P("grp", None, "tr"),
        check_vma=False,
    )
```

profile of v0, /device:TPU:1, one launch (start us, length us, event | category | flops | bytes accessed | tf_op | source)
XLA Modules:
  0.0 170.8 jit_solution(10598327211172347177)
XLA Ops:
  6.5 0.0 all-gather.2.cloned.1.call-start
  7.2 1.5 broadcast_select_fusion
  8.7 0.0 all-gather.2.cloned.1.call-update
  8.7 0.0 reduce-scatter.2.cloned.1.call-start
  8.7 86.8 %all-gather.2.cloned.1.call-done = bf16[512,1,2048]{2,0,1:T(8,128)(2,1)} async-done(((bf16[16,1,2048]{2,0,1:T(8,128)(2,1)}), bf16[512,1,2048]{2,0,1:T(8,128)(2,1)}) %all-gather.2.cloned.1.call-update) | async-done | bytes 2097168 | tf_op jit(solution)/shard_map/all_gather | solution.py:16
  95.6 6.2 %fusion.3 = f32[512,1,896]{2,0,1:T(8,128)} fusion(bf16[1,2048,896]{2,1,0:T(8,128)(2,1)} %param.4, bf16[512,1,2048]{2,0,1:T(8,128)(2,1)} %all-gather.2.cloned.1.call-done), kind=kOutput, calls=%fused_computation.3 | convolution fusion | flops 1879048192 | bytes 7602176 | tf_op jit(solution)/shard_map/inc,nca->ina/dot_general | solution.py:8
  101.8 0.0 reduce-scatter.2.cloned.1.call-update
  101.8 60.6 %reduce-scatter.2.cloned.1.call-done = f32[32,1,896]{2,0,1:T(8,128)} async-done(((f32[512,1,896]{2,0,1:T(8,128)}), f32[32,1,896]{2,0,1:T(8,128)}) %reduce-scatter.2.cloned.1.call-update) | async-done | bytes 114704 | tf_op jit(solution)/shard_map/reduce_scatter | solution.py:17
  162.4 1.5 convert_element_type.3
  (1 shorter events, 0.0 us)
Async XLA Ops:
  6.5 89.1 %all-gather.2.cloned.1.call-start = ((), (), s32[]{:S(2)}) async-start(), calls=%async_computation.1 | async-start | bytes 2162688 | tf_op jit(solution)/shard_map/all_gather | solution.py:16
  8.7 153.7 %reduce-scatter.2.cloned.1.call-start = ((), (), s32[]{:S(2)}) async-start(), calls=%async_computation.2 | async-start | bytes 1949696 | tf_op jit(solution)/shard_map/reduce_scatter | solution.py:17
Sparse Core Ops, SparseCore 0:
  10.5 85.0 all-gather.1
  102.0 60.3 reduce-scatter.1
where the time goes:
time: 173 us; the launch traced here: 171 us
  waiting for transfers between devices  147 us (85%)
  between operations  14.1 us (8%)
  matrix products  6.22 us (4%)
  other arithmetic  3 us (2%)
    all_gather x1, waiting for transfers between devices, on_device(): whole = lax.all_gather(masked, 'tr', axis=0, tiled=True)  86.8 us
    reduce_scatter x1, waiting for transfers between devices, on_device(): lax.psum_scatter(contract(whole, integrals), 'grp', scatter_dimension=0,...  60.6 us
    dot_general x1, matrix products, contract(): jnp.einsum('inc,nca->ina', rows, integrals, preferred_element_type=jnp.fl...  6.22 us
  transfers between devices with their start and end apart: 2, of which 2 were waited for; matrix products, arithmetic and copies ran while one was open for 0% of the time, Pallas kernels for 0%

commit v1 on v0

v1 whole, which is shorter than its diff:
```python
import jax
import jax.numpy as jnp
from jax import lax
from jax.sharding import PartitionSpec as P

X, Y, Z = 4, 8, 8
CLASSES = 4


def tr_of(x, y):
    return (x % X) * Y + y % Y


ORDER = [4 * h + 2 * k + b for k in range(2) for h in range(2) for b in range(2)]
CLASS_GROUPS = [[tr_of(c - 2 * y, y) for y in ORDER] for c in range(CLASSES)]


def z_groups():
    groups = []
    for core in range(2):
        for t in range(X * Y):
            c = (t // Y + 2 * (t % Y)) % CLASSES
            planes = [2 * ((c + d) % X) + h for d in range(CLASSES) for h in range(2)]
            groups.append([(2 * z + core) * X * Y + t for z in planes])
    return groups


Z_GROUPS = z_groups()


def from_neighbour(block, dx, dy):
    pairs = [(tr_of(t // Y + dx, t % Y + dy), t) for t in range(X * Y)]
    return lax.ppermute(block, "tr", pairs)


def on_device(amplitudes, integrals, slab_count):
    rows, _, depth = amplitudes.shape
    width = integrals.shape[2]
    column = lax.broadcasted_iota(jnp.int32, (rows, depth), 1)
    masked = jnp.where(column < slab_count[0, 0], amplitudes[:, 0, :], jnp.zeros((), amplitudes.dtype))
    copies = jnp.broadcast_to(masked[None], (8, rows, depth))
    own = lax.all_to_all(copies, "tr", 0, 0, axis_index_groups=CLASS_GROUPS)
    right = from_neighbour(own, 1, 0)
    left = from_neighbour(own, -1, 0)
    up = from_neighbour(own[:4], 0, 1)
    down = from_neighbour(own[4:], 0, -1)
    whole = jnp.concatenate([own[:4], right[:4], up, left[:4], own[4:], right[4:], down, left[4:]], axis=0)
    partial = jnp.dot(whole.reshape(32 * rows, depth), integrals[0], preferred_element_type=jnp.float32)
    both = lax.all_to_all(partial.reshape(2, 16 * rows, width), "grp", 0, 0, axis_index_groups=[[2 * z, 2 * z + 1] for z in range(Z)])
    chip = (both[0] + both[1]).reshape(CLASSES, 2, 2, rows, width)
    second = jnp.concatenate([chip[2:, :, 1], chip[:2, :, 1]], axis=0)
    chip = jnp.stack([chip[:, :, 0], second], axis=2).reshape(Z, 2 * rows, width)
    summed = lax.all_to_all(chip, ("grp", "tr"), 0, 0, axis_index_groups=Z_GROUPS).sum(axis=0)
    return summed.astype(jnp.bfloat16)[:, None, :]


def solution(mesh):
    return jax.shard_map(
        on_device,
        mesh=mesh,
        in_specs=(P("tr", None, "grp"), P(None, "grp", "tr"), P(None, "grp")),
        out_specs=P("grp", None, "tr"),
        check_vma=False,
    )
```

time: 173 us -> 97.5 us (0.56)
  waiting for transfers between devices: 147 us -> 12.6 us
  blocking collectives: 0 us -> 68.1 us
  between operations: 14.1 us -> 0.83 us
  starting transfers between devices: 0.04 us -> 11 us
  matrix products: 6.22 us -> 2.33 us
    all_gather x1 -> x0, waiting for transfers between devices: 86.8 us -> none  [on_device(): whole = lax.all_gather(masked, 'tr', axis=0, tiled=True)]
    all_to_all x0 -> x3, blocking collectives: none -> 68.1 us  [the longest x1 34.9 us: on_device(): lax.all_to_all(chip, ('grp', 'tr'), 0, 0, axis_index_groups=Z_GROUPS)]
    reduce_scatter x1 -> x0, waiting for transfers between devices: 60.6 us -> none  [on_device(): lax.psum_scatter(contract(whole, integrals), 'grp', scatter_dimension=0,...]
    ppermute x0 -> x4, waiting for transfers between devices: none -> 12.6 us  [from_neighbour(): return lax.ppermute(block, 'tr', pairs)]
    ppermute x0 -> x4, starting transfers between devices: none -> 11 us  [from_neighbour(): return lax.ppermute(block, 'tr', pairs)]
    dot_general x1, matrix products: 6.22 us -> 2.33 us  [on_device(): jnp.dot(whole.reshape(32 * rows, depth), integrals[0], preferred_element_...]
  transfers between devices with their start and end apart: 2 -> 4, of which waited for: 2 -> 2; matrix products, arithmetic and copies ran while one was open for 0% -> 0% of each run, Pallas kernels for 0% -> 0%
where the time goes in v1:
time: 97.5 us; the launch traced here: 96.9 us
  blocking collectives  68.1 us (70%)
  waiting for transfers between devices  12.6 us (13%)
  starting transfers between devices  11 us (11%)
  matrix products  2.33 us (2%)
  other arithmetic  1.72 us (2%)
    all_to_all x1, blocking collectives, on_device(): lax.all_to_all(chip, ('grp', 'tr'), 0, 0, axis_index_groups=Z_GROUPS)  34.9 us
    all_to_all x1, blocking collectives, on_device(): own = lax.all_to_all(copies, 'tr', 0, 0, axis_index_groups=CLASS_GROUPS)  25.4 us
    ppermute x4, waiting for transfers between devices, from_neighbour(): return lax.ppermute(block, 'tr', pairs)  12.6 us
    ppermute x4, starting transfers between devices, from_neighbour(): return lax.ppermute(block, 'tr', pairs)  11 us
    all_to_all x1, blocking collectives, on_device(): lax.all_to_all(partial.reshape(2, 16 * rows, width), 'grp', 0, 0, axis_in...  7.7 us
    dot_general x1, matrix products, on_device(): jnp.dot(whole.reshape(32 * rows, depth), integrals[0], preferred_element_...  2.33 us
  transfers between devices with their start and end apart: 4, of which 2 were waited for; matrix products, arithmetic and copies ran while one was open for 0% of the time, Pallas kernels for 0%

profile of v1, /device:TPU:1, one launch (start us, length us, event | category | flops | bytes accessed | tf_op | source)
XLA Modules:
  0.0 96.9 jit_solution(8086816997933843994)
XLA Ops:
  0.7 0.9 bitcast_select_fusion
  1.6 25.4 %all_to_all.15 = bf16[8,16,2048]{2,1,0:T(8,128)(2,1)S(1)} all-to-all(bf16[8,16,2048]{2,1,0:T(8,128)(2,1)S(1)} %broadcast_in_dim.12), channel_id=1, replica_groups={{0,17,4,21,2,19,6,23},{8,25,12,29,10,27,14,31},{16,1,20,5,18,3,22,7},{2..., dimensions={0} | all-to-all | bytes 1048576 | tf_op jit(solution)/shard_map/all_to_all | solution.py:42
  27.0 3.6 %collective-permute-start = (bf16[8,16,2048]{2,1,0:T(8,128)(2,1)S(1)}, bf16[8,16,2048]{2,1,0:T(8,128)(2,1)S(1)}, u32[]{:S(2)}, u32[]{:S(2)}) collective-permute-start(bf16[8,16,2048]{2,1,0:T(8,128)(2,1)S(1)} %all_to_all.15), channel_id=1, source_target_pairs={{8,0},{9,1},{10,2},{11,3},{12,4},{13,5},{14,6},{15,7},{16,8},{17,9... | collective-permute-start | bytes 1572872 | tf_op jit(solution)/shard_map/ppermute | solution.py:33
  30.6 0.1 fusion.2
  30.6 0.0 copy-start
  30.6 2.2 %collective-permute-start.1 = (bf16[4,16,2048]{2,1,0:T(8,128)(2,1)S(1)}, bf16[4,16,2048]{2,1,0:T(8,128)(2,1)S(1)}, u32[]{:S(2)}, u32[]{:S(2)}) collective-permute-start(bf16[4,16,2048]{2,1,0:T(8,128)(2,1)S(1)} %get-tuple-element.9), channel_id=1, source_target_pairs={{1,0},{2,1},{3,2},{4,3},{5,4},{6,5},{7,6},{0,7},{9,8},{10,9},{11,1... | collective-permute-start | bytes 786440 | tf_op jit(solution)/shard_map/ppermute | solution.py:33
  32.8 3.4 %collective-permute-start.3 = (bf16[4,16,2048]{2,1,0:T(8,128)(2,1)S(1)}, bf16[4,16,2048]{2,1,0:T(8,128)(2,1)S(1)}, u32[]{:S(2)}, u32[]{:S(2)}) collective-permute-start(bf16[4,16,2048]{2,1,0:T(8,128)(2,1)S(1)} %get-tuple-element.7), channel_id=1, source_target_pairs={{7,0},{0,1},{1,2},{2,3},{3,4},{4,5},{5,6},{6,7},{15,8},{8,9},{9,10... | collective-permute-start | bytes 786440 | tf_op jit(solution)/shard_map/ppermute | solution.py:33
  36.2 1.9 %collective-permute-start.2 = (bf16[8,16,2048]{2,1,0:T(8,128)(2,1)S(1)}, bf16[8,16,2048]{2,1,0:T(8,128)(2,1)S(1)}, u32[]{:S(2)}, u32[]{:S(2)}) collective-permute-start(bf16[8,16,2048]{2,1,0:T(8,128)(2,1)S(1)} %all_to_all.15), channel_id=1, source_target_pairs={{24,0},{25,1},{26,2},{27,3},{28,4},{29,5},{30,6},{31,7},{0,8},{1,9... | collective-permute-start | bytes 1572872 | tf_op jit(solution)/shard_map/ppermute | solution.py:33
  38.1 2.5 %collective-permute-done = bf16[8,16,2048]{2,1,0:T(8,128)(2,1)S(1)} collective-permute-done((bf16[8,16,2048]{2,1,0:T(8,128)(2,1)S(1)}, bf16[8,16,2048]{2,1,0:T(8,128)(2,1)S(1)}, u32[]{:S(2)}, u32[]{:S(2)}) %collective-permute-start) | collective-permute-done | bytes 524320 | tf_op jit(solution)/shard_map/ppermute | solution.py:33
  40.7 0.0 collective-permute-done.1
  40.7 10.1 %collective-permute-done.2 = bf16[8,16,2048]{2,1,0:T(8,128)(2,1)S(1)} collective-permute-done((bf16[8,16,2048]{2,1,0:T(8,128)(2,1)S(1)}, bf16[8,16,2048]{2,1,0:T(8,128)(2,1)S(1)}, u32[]{:S(2)}, u32[]{:S(2)}) %collective-permute-start.2) | collective-permute-done | bytes 524320 | tf_op jit(solution)/shard_map/ppermute | solution.py:33
  50.9 0.0 collective-permute-done.3
  50.9 0.0 copy-done
  50.9 2.3 %fusion = f32[2,256,896]{2,1,0:T(8,128)S(1)} fusion(bf16[2,256,2048]{2,1,0:T(8,128)(2,1)S(1)} %bitcast.28, bf16[1,2048,896]{2,1,0:T(8,128)(2,1)S(1)} %copy-done), kind=kOutput, calls=%fused_computation | convolution fusion | flops 1879048192 | bytes 7602176 | tf_op jit(solution)/shard_map/dot_general | solution.py:48
  53.3 7.7 %all_to_all.16 = f32[2,256,896]{2,1,0:T(8,128)S(1)} all-to-all(f32[2,256,896]{2,1,0:T(8,128)S(1)} %fusion), channel_id=1, replica_groups={{0,32},{64,96},{128,160},{192,224},{256,288},{320,352},{384,416},{448,4..., dimensions={0} | all-to-all | bytes 3670016 | tf_op jit(solution)/shard_map/all_to_all | solution.py:49
  61.0 0.1 slice_add_fusion
  61.2 0.1 pad_maximum_fusion
  61.3 34.9 %all_to_all.17 = f32[8,32,896]{2,1,0:T(8,128)S(1)} all-to-all(f32[8,32,896]{2,1,0:T(8,128)S(1)} %bitcast.25), channel_id=1, replica_groups={{0,64,128,192,256,320,384,448},{257,321,385,449,1,65,129,193},{2,66,130..., dimensions={0} | all-to-all | bytes 1835008 | tf_op jit(solution)/shard_map/all_to_all | solution.py:53
  96.2 0.7 reduce_sum.9
  (12 shorter events, 0.3 us)
Async XLA Ops:
  27.0 13.7 %collective-permute-start = (bf16[8,16,2048]{2,1,0:T(8,128)(2,1)S(1)}, bf16[8,16,2048]{2,1,0:T(8,128)(2,1)S(1)}, u32[]{:S(2)}, u32[]{:S(2)}) collective-permute-start(bf16[8,16,2048]{2,1,0:T(8,128)(2,1)S(1)} %all_to_all.15), channel_id=1, source_target_pairs={{8,0},{9,1},{10,2},{11,3},{12,4},{13,5},{14,6},{15,7},{16,8},{17,9... | collective-permute-start | bytes 1572872 | tf_op jit(solution)/shard_map/ppermute | solution.py:33
  30.6 20.3 %copy-start = (bf16[1,2048,896]{2,1,0:T(8,128)(2,1)S(1)}, bf16[1,2048,896]{2,1,0:T(8,128)(2,1)}, u32[]{:S(2)}) copy-start(bf16[1,2048,896]{2,1,0:T(8,128)(2,1)} %param.4) | copy-start | bytes 11010052
  30.6 10.0 %collective-permute-start.1 = (bf16[4,16,2048]{2,1,0:T(8,128)(2,1)S(1)}, bf16[4,16,2048]{2,1,0:T(8,128)(2,1)S(1)}, u32[]{:S(2)}, u32[]{:S(2)}) collective-permute-start(bf16[4,16,2048]{2,1,0:T(8,128)(2,1)S(1)} %get-tuple-element.9), channel_id=1, source_target_pairs={{1,0},{2,1},{3,2},{4,3},{5,4},{6,5},{7,6},{0,7},{9,8},{10,9},{11,1... | collective-permute-start | bytes 786440 | tf_op jit(solution)/shard_map/ppermute | solution.py:33
  32.8 18.0 %collective-permute-start.3 = (bf16[4,16,2048]{2,1,0:T(8,128)(2,1)S(1)}, bf16[4,16,2048]{2,1,0:T(8,128)(2,1)S(1)}, u32[]{:S(2)}, u32[]{:S(2)}) collective-permute-start(bf16[4,16,2048]{2,1,0:T(8,128)(2,1)S(1)} %get-tuple-element.7), channel_id=1, source_target_pairs={{7,0},{0,1},{1,2},{2,3},{3,4},{4,5},{5,6},{6,7},{15,8},{8,9},{9,10... | collective-permute-start | bytes 786440 | tf_op jit(solution)/shard_map/ppermute | solution.py:33
  36.2 14.6 %collective-permute-start.2 = (bf16[8,16,2048]{2,1,0:T(8,128)(2,1)S(1)}, bf16[8,16,2048]{2,1,0:T(8,128)(2,1)S(1)}, u32[]{:S(2)}, u32[]{:S(2)}) collective-permute-start(bf16[8,16,2048]{2,1,0:T(8,128)(2,1)S(1)} %all_to_all.15), channel_id=1, source_target_pairs={{24,0},{25,1},{26,2},{27,3},{28,4},{29,5},{30,6},{31,7},{0,8},{1,9... | collective-permute-start | bytes 1572872 | tf_op jit(solution)/shard_map/ppermute | solution.py:33

commit v2 on v1

--- a/solution.py
+++ b/solution.py
@@ -44,12 +44,17 @@
     left = from_neighbour(own, -1, 0)
     up = from_neighbour(own[:4], 0, 1)
     down = from_neighbour(own[4:], 0, -1)
-    whole = jnp.concatenate([own[:4], right[:4], up, left[:4], own[4:], right[4:], down, left[4:]], axis=0)
-    partial = jnp.dot(whole.reshape(32 * rows, depth), integrals[0], preferred_element_type=jnp.float32)
-    both = lax.all_to_all(partial.reshape(2, 16 * rows, width), "grp", 0, 0, axis_index_groups=[[2 * z, 2 * z + 1] for z in range(Z)])
-    chip = (both[0] + both[1]).reshape(CLASSES, 2, 2, rows, width)
-    second = jnp.concatenate([chip[2:, :, 1], chip[:2, :, 1]], axis=0)
-    chip = jnp.stack([chip[:, :, 0], second], axis=2).reshape(Z, 2 * rows, width)
+    mine = lax.rem(lax.axis_index("grp"), 2)
+
+    core0 = mine == 0
+    whole = jnp.concatenate([own, right, left, up, down], axis=0).reshape(-1, depth)
+    partial = jnp.dot(whole, integrals[0], preferred_element_type=jnp.float32)
+    partial = partial.reshape(CLASSES, 2, 4 * rows, width)
+    given = lax.ppermute(jnp.where(core0, partial[:, 1], partial[:, 0]), "grp", [(g, g ^ 1) for g in range(2 * Z)])
+    total = jnp.where(core0, partial[:, 0], partial[:, 1]) + given
+    chip = [total[i].reshape(2, 2, rows, width) for i in (0, 1, 3, 2)]
+    paired = [jnp.stack([chip[d][:, 0], chip[(d + 2) % CLASSES][:, 1]], axis=1) for d in range(CLASSES)]
+    chip = jnp.stack(paired).reshape(Z, 2 * rows, width)
     summed = lax.all_to_all(chip, ("grp", "tr"), 0, 0, axis_index_groups=Z_GROUPS).sum(axis=0)
     return summed.astype(jnp.bfloat16)[:, None, :]
 

time: 97.5 us -> 92.5 us (0.949)
  blocking collectives: 68.1 us -> 34.9 us
  waiting for transfers between devices: 12.6 us -> 27.1 us
  starting transfers between devices: 11 us -> 23.8 us
    all_to_all x2 -> x0, blocking collectives: 33.1 us -> none  [the longest x1 25.4 us: on_device(): own = lax.all_to_all(copies, 'tr', 0, 0, axis_index_groups=CLASS_GROUPS)]
    all_to_all x0 -> x1, waiting for transfers between devices: none -> 16.9 us  [on_device(): own = lax.all_to_all(copies, 'tr', 0, 0, axis_index_groups=CLASS_GROUPS)]
    all_to_all x0 -> x1, starting transfers between devices: none -> 9.33 us  [on_device(): own = lax.all_to_all(copies, 'tr', 0, 0, axis_index_groups=CLASS_GROUPS)]
    ppermute x4, waiting for transfers between devices: 12.6 us -> 8.08 us  [from_neighbour(): return lax.ppermute(block, 'tr', pairs)]
    ppermute x0 -> x1, starting transfers between devices: none -> 3.64 us  [on_device(): lax.ppermute(jnp.where(core0, partial[:, 1], partial[:, 0]), 'grp', [(g,...]
    ppermute x0 -> x1, waiting for transfers between devices: none -> 2.08 us  [on_device(): lax.ppermute(jnp.where(core0, partial[:, 1], partial[:, 0]), 'grp', [(g,...]
  transfers between devices with their start and end apart: 4 -> 6, of which waited for: 2 -> 4; matrix products, arithmetic and copies ran while one was open for 0% -> 0% of each run, Pallas kernels for 0% -> 0%
where the time goes in v2:
time: 92.5 us; the launch traced here: 92.1 us
  blocking collectives  34.9 us (38%)
  waiting for transfers between devices  27.1 us (29%)
  starting transfers between devices  23.8 us (26%)
  matrix products  2.33 us (3%)
  other arithmetic  1.88 us (2%)
  local copies, waits for them, and re-layouts  1.17 us (1%)
    all_to_all x1, blocking collectives, on_device(): lax.all_to_all(chip, ('grp', 'tr'), 0, 0, axis_index_groups=Z_GROUPS)  34.9 us
    all_to_all x1, waiting for transfers between devices, on_device(): own = lax.all_to_all(copies, 'tr', 0, 0, axis_index_groups=CLASS_GROUPS)  16.9 us
    ppermute x4, starting transfers between devices, from_neighbour(): return lax.ppermute(block, 'tr', pairs)  10.9 us
    all_to_all x1, starting transfers between devices, on_device(): own = lax.all_to_all(copies, 'tr', 0, 0, axis_index_groups=CLASS_GROUPS)  9.33 us
    ppermute x4, waiting for transfers between devices, from_neighbour(): return lax.ppermute(block, 'tr', pairs)  8.08 us
    ppermute x1, starting transfers between devices, on_device(): lax.ppermute(jnp.where(core0, partial[:, 1], partial[:, 0]), 'grp', [(g,...  3.64 us
    dot_general x1, matrix products, on_device(): partial = jnp.dot(whole, integrals[0], preferred_element_type=jnp.float32)  2.33 us
    ppermute x1, waiting for transfers between devices, on_device(): lax.ppermute(jnp.where(core0, partial[:, 1], partial[:, 0]), 'grp', [(g,...  2.08 us
  transfers between devices with their start and end apart: 6, of which 4 were waited for; matrix products, arithmetic and copies ran while one was open for 0% of the time, Pallas kernels for 0%

profile of v2, /device:TPU:1, one launch (start us, length us, event | category | flops | bytes accessed | tf_op | source)
XLA Modules:
  0.0 92.1 jit_solution(4192737922444111643)
XLA Ops:
  0.7 0.9 bitcast_select_fusion.1
  1.5 0.8 broadcast_in_dim.12
  2.4 9.3 %all-to-all-start = ((bf16[8,16,2048]{2,1,0:T(8,128)(2,1)}), bf16[8,16,2048]{2,1,0:T(8,128)(2,1)S(1)}, u32[]{:S(2)}, u32[]{:S(2)}) async-start(bf16[8,16,2048]{2,1,0:T(8,128)(2,1)} %broadcast_in_dim.12), calls=%async_computation | async-start | bytes 1048576 | tf_op jit(solution)/shard_map/all_to_all | solution.py:42
  11.7 16.9 %all-to-all-done = bf16[8,16,2048]{2,1,0:T(8,128)(2,1)S(1)} async-done(((bf16[8,16,2048]{2,1,0:T(8,128)(2,1)}), bf16[8,16,2048]{2,1,0:T(8,128)(2,1)S(1)}, u32[]{:S(2)}, u32[]{:S(2)}) %all-to-all-start) | async-done | bytes 524320 | tf_op jit(solution)/shard_map/all_to_all | solution.py:42
  28.6 3.4 %collective-permute-start = (bf16[8,16,2048]{2,1,0:T(8,128)(2,1)S(1)}, bf16[8,16,2048]{2,1,0:T(8,128)(2,1)S(1)}, u32[]{:S(2)}, u32[]{:S(2)}) collective-permute-start(bf16[8,16,2048]{2,1,0:T(8,128)(2,1)S(1)} %all-to-all-done), channel_id=1, source_target_pairs={{8,0},{9,1},{10,2},{11,3},{12,4},{13,5},{14,6},{15,7},{16,8},{17,9... | collective-permute-start | bytes 1572872 | tf_op jit(solution)/shard_map/ppermute | solution.py:33
  32.1 1.9 %collective-permute-start.1 = (bf16[8,16,2048]{2,1,0:T(8,128)(2,1)S(1)}, bf16[8,16,2048]{2,1,0:T(8,128)(2,1)S(1)}, u32[]{:S(2)}, u32[]{:S(2)}) collective-permute-start(bf16[8,16,2048]{2,1,0:T(8,128)(2,1)S(1)} %all-to-all-done), channel_id=1, source_target_pairs={{24,0},{25,1},{26,2},{27,3},{28,4},{29,5},{30,6},{31,7},{0,8},{1,9... | collective-permute-start | bytes 1572872 | tf_op jit(solution)/shard_map/ppermute | solution.py:33
  34.0 1.9 %collective-permute-start.2 = (bf16[4,16,2048]{2,1,0:T(8,128)(2,1)S(1)}, bf16[4,16,2048]{2,1,0:T(8,128)(2,1)S(1)}, u32[]{:S(2)}, u32[]{:S(2)}) collective-permute-start(bf16[4,16,2048]{2,1,0:T(8,128)(2,1)S(1)} %get-tuple-element.10), channel_id=1, source_target_pairs={{1,0},{2,1},{3,2},{4,3},{5,4},{6,5},{7,6},{0,7},{9,8},{10,9},{11,1... | collective-permute-start | bytes 786440 | tf_op jit(solution)/shard_map/ppermute | solution.py:33
  36.0 0.0 copy-start
  36.0 3.6 %collective-permute-start.3 = (bf16[4,16,2048]{2,1,0:T(8,128)(2,1)S(1)}, bf16[4,16,2048]{2,1,0:T(8,128)(2,1)S(1)}, u32[]{:S(2)}, u32[]{:S(2)}) collective-permute-start(bf16[4,16,2048]{2,1,0:T(8,128)(2,1)S(1)} %get-tuple-element.9), channel_id=1, source_target_pairs={{7,0},{0,1},{1,2},{2,3},{3,4},{4,5},{5,6},{6,7},{15,8},{8,9},{9,10... | collective-permute-start | bytes 786440 | tf_op jit(solution)/shard_map/ppermute | solution.py:33
  39.7 3.9 %collective-permute-done = bf16[8,16,2048]{2,1,0:T(8,128)(2,1)S(1)} collective-permute-done((bf16[8,16,2048]{2,1,0:T(8,128)(2,1)S(1)}, bf16[8,16,2048]{2,1,0:T(8,128)(2,1)S(1)}, u32[]{:S(2)}, u32[]{:S(2)}) %collective-permute-start) | collective-permute-done | bytes 524320 | tf_op jit(solution)/shard_map/ppermute | solution.py:33
  43.6 4.2 %collective-permute-done.1 = bf16[8,16,2048]{2,1,0:T(8,128)(2,1)S(1)} collective-permute-done((bf16[8,16,2048]{2,1,0:T(8,128)(2,1)S(1)}, bf16[8,16,2048]{2,1,0:T(8,128)(2,1)S(1)}, u32[]{:S(2)}, u32[]{:S(2)}) %collective-permute-start.1) | collective-permute-done | bytes 524320 | tf_op jit(solution)/shard_map/ppermute | solution.py:33
  47.8 0.0 collective-permute-done.2
  47.9 0.0 collective-permute-done.3
  47.9 0.0 copy-done
  47.9 2.3 %fusion = f32[4,2,64,896]{3,2,1,0:T(8,128)S(1)} fusion(bf16[4,2,64,2048]{3,2,1,0:T(8,128)(2,1)S(1)} %bitcast.52, bf16[1,2048,896]{2,1,0:T(8,128)(2,1)S(1)} %copy-done), kind=kOutput, calls=%fused_computation | convolution fusion | flops 1879048192 | bytes 7602176 | tf_op jit(solution)/shard_map/dot_general | solution.py:51
  50.2 0.1 select_bitcast_fusion
  50.3 3.6 %collective-permute-start.4 = (f32[4,64,896]{2,1,0:T(8,128)S(1)}, f32[4,64,896]{2,1,0:T(8,128)S(1)}, u32[]{:S(2)}, u32[]{:S(2)}) collective-permute-start(f32[4,64,896]{2,1,0:T(8,128)S(1)} %select_bitcast_fusion), channel_id=1, source_target_pairs={{0,32},{32,0},{64,96},{96,64},{128,160},{160,128},{192,224},{224,1... | collective-permute-start | bytes 2752520 | tf_op jit(solution)/shard_map/ppermute | solution.py:53
  54.0 2.1 %collective-permute-done.4 = f32[4,64,896]{2,1,0:T(8,128)S(1)} collective-permute-done((f32[4,64,896]{2,1,0:T(8,128)S(1)}, f32[4,64,896]{2,1,0:T(8,128)S(1)}, u32[]{:S(2)}, u32[]{:S(2)}) %collective-permute-start.4) | collective-permute-done | bytes 917536 | tf_op jit(solution)/shard_map/ppermute | solution.py:53
  56.1 0.1 fusion.3
  56.2 0.1 fusion.4
  56.4 0.1 pad_maximum_fusion
  56.5 34.9 %all_to_all.10 = f32[8,32,896]{2,1,0:T(8,128)S(1)} all-to-all(f32[8,32,896]{2,1,0:T(8,128)S(1)} %bitcast.47), channel_id=1, replica_groups={{0,64,128,192,256,320,384,448},{257,321,385,449,1,65,129,193},{2,66,130..., dimensions={0} | all-to-all | bytes 1835008 | tf_op jit(solution)/shard_map/all_to_all | solution.py:58
  91.5 0.7 reduce_sum.9
  (13 shorter events, 0.3 us)
Async XLA Ops:
  2.4 26.3 %all-to-all-start = ((bf16[8,16,2048]{2,1,0:T(8,128)(2,1)}), bf16[8,16,2048]{2,1,0:T(8,128)(2,1)S(1)}, u32[]{:S(2)}, u32[]{:S(2)}) async-start(bf16[8,16,2048]{2,1,0:T(8,128)(2,1)} %broadcast_in_dim.12), calls=%async_computation | async-start | bytes 1048576 | tf_op jit(solution)/shard_map/all_to_all | solution.py:42
  28.6 14.9 %collective-permute-start = (bf16[8,16,2048]{2,1,0:T(8,128)(2,1)S(1)}, bf16[8,16,2048]{2,1,0:T(8,128)(2,1)S(1)}, u32[]{:S(2)}, u32[]{:S(2)}) collective-permute-start(bf16[8,16,2048]{2,1,0:T(8,128)(2,1)S(1)} %all-to-all-done), channel_id=1, source_target_pairs={{8,0},{9,1},{10,2},{11,3},{12,4},{13,5},{14,6},{15,7},{16,8},{17,9... | collective-permute-start | bytes 1572872 | tf_op jit(solution)/shard_map/ppermute | solution.py:33
  32.1 15.7 %collective-permute-start.1 = (bf16[8,16,2048]{2,1,0:T(8,128)(2,1)S(1)}, bf16[8,16,2048]{2,1,0:T(8,128)(2,1)S(1)}, u32[]{:S(2)}, u32[]{:S(2)}) collective-permute-start(bf16[8,16,2048]{2,1,0:T(8,128)(2,1)S(1)} %all-to-all-done), channel_id=1, source_target_pairs={{24,0},{25,1},{26,2},{27,3},{28,4},{29,5},{30,6},{31,7},{0,8},{1,9... | collective-permute-start | bytes 1572872 | tf_op jit(solution)/shard_map/ppermute | solution.py:33
  34.0 13.8 %collective-permute-start.2 = (bf16[4,16,2048]{2,1,0:T(8,128)(2,1)S(1)}, bf16[4,16,2048]{2,1,0:T(8,128)(2,1)S(1)}, u32[]{:S(2)}, u32[]{:S(2)}) collective-permute-start(bf16[4,16,2048]{2,1,0:T(8,128)(2,1)S(1)} %get-tuple-element.10), channel_id=1, source_target_pairs={{1,0},{2,1},{3,2},{4,3},{5,4},{6,5},{7,6},{0,7},{9,8},{10,9},{11,1... | collective-permute-start | bytes 786440 | tf_op jit(solution)/shard_map/ppermute | solution.py:33
  36.0 11.9 %copy-start = (bf16[1,2048,896]{2,1,0:T(8,128)(2,1)S(1)}, bf16[1,2048,896]{2,1,0:T(8,128)(2,1)}, u32[]{:S(2)}) copy-start(bf16[1,2048,896]{2,1,0:T(8,128)(2,1)} %param.4) | copy-start | bytes 11010052
  36.0 11.9 %collective-permute-start.3 = (bf16[4,16,2048]{2,1,0:T(8,128)(2,1)S(1)}, bf16[4,16,2048]{2,1,0:T(8,128)(2,1)S(1)}, u32[]{:S(2)}, u32[]{:S(2)}) collective-permute-start(bf16[4,16,2048]{2,1,0:T(8,128)(2,1)S(1)} %get-tuple-element.9), channel_id=1, source_target_pairs={{7,0},{0,1},{1,2},{2,3},{3,4},{4,5},{5,6},{6,7},{15,8},{8,9},{9,10... | collective-permute-start | bytes 786440 | tf_op jit(solution)/shard_map/ppermute | solution.py:33
  50.3 5.7 %collective-permute-start.4 = (f32[4,64,896]{2,1,0:T(8,128)S(1)}, f32[4,64,896]{2,1,0:T(8,128)S(1)}, u32[]{:S(2)}, u32[]{:S(2)}) collective-permute-start(f32[4,64,896]{2,1,0:T(8,128)S(1)} %select_bitcast_fusion), channel_id=1, source_target_pairs={{0,32},{32,0},{64,96},{96,64},{128,160},{160,128},{192,224},{224,1... | collective-permute-start | bytes 2752520 | tf_op jit(solution)/shard_map/ppermute | solution.py:53

commit v3 on v2

--- a/solution.py
+++ b/solution.py
@@ -1,6 +1,8 @@
 import jax
 import jax.numpy as jnp
 from jax import lax
+from jax.experimental import pallas as pl
+from jax.experimental.pallas import tpu as pltpu
 from jax.sharding import PartitionSpec as P
 
 X, Y, Z = 4, 8, 8
@@ -33,6 +35,50 @@
     return lax.ppermute(block, "tr", pairs)
 
 
+def pack(ours_ref, given_ref, out_ref):
+    lanes = out_ref.shape[2]
+    rows = ours_ref.shape[3]
+    groups = ours_ref.shape[4] // lanes
+    slot = (0, 1, 3, 2)
+    for d in range(CLASSES):
+        for h in range(2):
+            exponents = []
+            for b in range(2):
+                at = (slot[(d + 2 * b) % CLASSES], h, b)
+                value = ours_ref[at] + given_ref[at]
+                top = jnp.max(jnp.abs(value), axis=1, keepdims=True)
+                exponent = jnp.ceil(jnp.log2(jnp.maximum(top, 2.0**-100)))
+                scaled = jnp.clip(jnp.round(value * jnp.exp2(15.0 - exponent)), -32767.0, 32767.0)
+                number = scaled.astype(jnp.int32).astype(jnp.int16)
+                for g in range(groups):
+                    out_ref[2 * d + h, pl.ds((2 * g + b) * rows, rows), :] = number[:, g * lanes : (g + 1) * lanes]
+                exponents.append(jnp.broadcast_to(exponent, (rows, lanes)))
+            lower = lax.broadcasted_iota(jnp.int32, (rows, lanes), 1) < lanes // 2
+            both = jnp.where(lower, exponents[0], exponents[1])
+            out_ref[2 * d + h, pl.ds(2 * groups * rows, rows), :] = both.astype(jnp.int32).astype(jnp.int16)
+
+
+def unpack_sum(in_ref, out_ref):
+    planes, _, lanes = in_ref.shape
+    rows = out_ref.shape[0] // 2
+    groups = out_ref.shape[1] // lanes
+    steps = []
+    for p in range(planes):
+        exponent = in_ref[p, pl.ds(2 * groups * rows, rows), :].astype(jnp.int32).astype(jnp.float32)
+        step = jnp.exp2(exponent - 15.0)
+        steps.append((step[:, :1], step[:, lanes // 2 : lanes // 2 + 1]))
+    for b in range(2):
+        for g in range(groups):
+            total = jnp.zeros((rows, lanes), jnp.float32)
+            for p in range(planes):
+                number = in_ref[p, pl.ds((2 * g + b) * rows, rows), :].astype(jnp.int32).astype(jnp.float32)
+                total += number * steps[p][b]
+            out_ref[pl.ds(b * rows, rows), g * lanes : (g + 1) * lanes] = total.astype(out_ref.dtype)
+
+
+LANES = 128
+
+
 def on_device(amplitudes, integrals, slab_count):
     rows, _, depth = amplitudes.shape
     width = integrals.shape[2]
@@ -51,12 +97,27 @@
     partial = jnp.dot(whole, integrals[0], preferred_element_type=jnp.float32)
     partial = partial.reshape(CLASSES, 2, 4 * rows, width)
     given = lax.ppermute(jnp.where(core0, partial[:, 1], partial[:, 0]), "grp", [(g, g ^ 1) for g in range(2 * Z)])
-    total = jnp.where(core0, partial[:, 0], partial[:, 1]) + given
-    chip = [total[i].reshape(2, 2, rows, width) for i in (0, 1, 3, 2)]
-    paired = [jnp.stack([chip[d][:, 0], chip[(d + 2) % CLASSES][:, 1]], axis=1) for d in range(CLASSES)]
-    chip = jnp.stack(paired).reshape(Z, 2 * rows, width)
-    summed = lax.all_to_all(chip, ("grp", "tr"), 0, 0, axis_index_groups=Z_GROUPS).sum(axis=0)
-    return summed.astype(jnp.bfloat16)[:, None, :]
+    ours = jnp.where(core0, partial[:, 0], partial[:, 1])
+    shape = (CLASSES, 2, 2, rows, width)
+    vmem = pl.BlockSpec(memory_space=pltpu.VMEM)
+    packed = pl.pallas_call(
+        pack,
+        out_shape=jax.ShapeDtypeStruct((Z, 2 * rows * (width // LANES) + rows, LANES), jnp.int16),
+        in_specs=[vmem, vmem],
+        out_specs=vmem,
+        compiler_params=pltpu.CompilerParams(vmem_limit_bytes=4 << 20),
+        name="pack",
+    )(ours.reshape(shape), given.reshape(shape))
+    arrived = lax.all_to_all(packed, ("grp", "tr"), 0, 0, axis_index_groups=Z_GROUPS)
+    ladder = pl.pallas_call(
+        unpack_sum,
+        out_shape=jax.ShapeDtypeStruct((2 * rows, width), jnp.bfloat16),
+        in_specs=[vmem],
+        out_specs=vmem,
+        compiler_params=pltpu.CompilerParams(vmem_limit_bytes=2 << 20),
+        name="unpack_sum",
+    )(arrived)
+    return ladder[:, None, :]
 
 
 def solution(mesh):

time: 92.5 us -> 83.3 us (0.901)
  blocking collectives: 34.9 us -> 25.7 us
  Pallas kernels: 0 us -> 1.07 us
    all_to_all x1, blocking collectives: 34.9 us -> 25.7 us  [on_device(): lax.all_to_all(packed, ('grp', 'tr'), 0, 0, axis_index_groups=Z_GROUPS)]
    pallas_call x0 -> x2, Pallas kernels: none -> 1.07 us  [the longest x1 0.77 us: on_device(): pl.pallas_call(unpack_sum, out_shape=jax.ShapeDtypeStruct((2 * rows, widt...]
where the time goes in v3:
time: 83.3 us; the launch traced here: 82.9 us
  waiting for transfers between devices  27.1 us (33%)
  blocking collectives  25.7 us (31%)
  starting transfers between devices  23.8 us (29%)
  matrix products  2.33 us (3%)
  Pallas kernels  1.07 us (1%)
  local copies, waits for them, and re-layouts  1.04 us (1%)
  other arithmetic  1.01 us (1%)
    all_to_all x1, blocking collectives, on_device(): lax.all_to_all(packed, ('grp', 'tr'), 0, 0, axis_index_groups=Z_GROUPS)  25.7 us
    all_to_all x1, waiting for transfers between devices, on_device(): own = lax.all_to_all(copies, 'tr', 0, 0, axis_index_groups=CLASS_GROUPS)  16.9 us
    ppermute x4, starting transfers between devices, from_neighbour(): return lax.ppermute(block, 'tr', pairs)  10.9 us
    all_to_all x1, starting transfers between devices, on_device(): own = lax.all_to_all(copies, 'tr', 0, 0, axis_index_groups=CLASS_GROUPS)  9.33 us
    ppermute x4, waiting for transfers between devices, from_neighbour(): return lax.ppermute(block, 'tr', pairs)  8.08 us
    ppermute x1, starting transfers between devices, on_device(): lax.ppermute(jnp.where(core0, partial[:, 1], partial[:, 0]), 'grp', [(g,...  3.64 us
    dot_general x1, matrix products, on_device(): partial = jnp.dot(whole, integrals[0], preferred_element_type=jnp.float32)  2.33 us
    ppermute x1, waiting for transfers between devices, on_device(): lax.ppermute(jnp.where(core0, partial[:, 1], partial[:, 0]), 'grp', [(g,...  2.08 us
  transfers between devices with their start and end apart: 6, of which 4 were waited for; matrix products, arithmetic and copies ran while one was open for 0% of the time, Pallas kernels for 0%

profile of v3, /device:TPU:1, one launch (start us, length us, event | category | flops | bytes accessed | tf_op | source)
XLA Modules:
  0.0 82.9 jit_solution(9712511375926148442)
XLA Ops:
  0.7 0.9 %bitcast_select_fusion = bf16[16,2048]{1,0:T(8,128)(2,1)S(1)} fusion(bf16[16,1,2048]{2,0,1:T(8,128)(2,1)} %param.3, pred[2048]{0:T(1024)(128)(4,1)S(1)} %iota_compare_fusion), kind=kLoop, calls=%fused_computation.4 | loop fusion | flops 32768 | bytes 133120 | tf_op jit(solution)/shard_map/jit(_where)/select_n | solution.py:86
  1.5 0.8 %broadcast_in_dim.14 = bf16[8,16,2048]{2,1,0:T(8,128)(2,1)} broadcast(bf16[16,2048]{1,0:T(8,128)(2,1)S(1)} %bitcast_select_fusion), dimensions={1,2} | broadcast | bytes 589824 | tf_op jit(solution)/shard_map/broadcast_in_dim | solution.py:87
  2.4 9.3 %all-to-all-start = ((bf16[8,16,2048]{2,1,0:T(8,128)(2,1)}), bf16[8,16,2048]{2,1,0:T(8,128)(2,1)S(1)}, u32[]{:S(2)}, u32[]{:S(2)}) async-start(bf16[8,16,2048]{2,1,0:T(8,128)(2,1)} %broadcast_in_dim.14), calls=%async_computation | async-start | bytes 1048576 | tf_op jit(solution)/shard_map/all_to_all | solution.py:88
  11.7 16.9 %all-to-all-done = bf16[8,16,2048]{2,1,0:T(8,128)(2,1)S(1)} async-done(((bf16[8,16,2048]{2,1,0:T(8,128)(2,1)}), bf16[8,16,2048]{2,1,0:T(8,128)(2,1)S(1)}, u32[]{:S(2)}, u32[]{:S(2)}) %all-to-all-start) | async-done | bytes 524320 | tf_op jit(solution)/shard_map/all_to_all | solution.py:88
  28.6 3.4 %collective-permute-start = (bf16[8,16,2048]{2,1,0:T(8,128)(2,1)S(1)}, bf16[8,16,2048]{2,1,0:T(8,128)(2,1)S(1)}, u32[]{:S(2)}, u32[]{:S(2)}) collective-permute-start(bf16[8,16,2048]{2,1,0:T(8,128)(2,1)S(1)} %all-to-all-done), channel_id=1, source_target_pairs={{8,0},{9,1},{10,2},{11,3},{12,4},{13,5},{14,6},{15,7},{16,8},{17,9... | collective-permute-start | bytes 1572872 | tf_op jit(solution)/shard_map/ppermute | solution.py:35
  32.1 1.9 %collective-permute-start.1 = (bf16[8,16,2048]{2,1,0:T(8,128)(2,1)S(1)}, bf16[8,16,2048]{2,1,0:T(8,128)(2,1)S(1)}, u32[]{:S(2)}, u32[]{:S(2)}) collective-permute-start(bf16[8,16,2048]{2,1,0:T(8,128)(2,1)S(1)} %all-to-all-done), channel_id=1, source_target_pairs={{24,0},{25,1},{26,2},{27,3},{28,4},{29,5},{30,6},{31,7},{0,8},{1,9... | collective-permute-start | bytes 1572872 | tf_op jit(solution)/shard_map/ppermute | solution.py:35
  34.0 1.9 %collective-permute-start.2 = (bf16[4,16,2048]{2,1,0:T(8,128)(2,1)S(1)}, bf16[4,16,2048]{2,1,0:T(8,128)(2,1)S(1)}, u32[]{:S(2)}, u32[]{:S(2)}) collective-permute-start(bf16[4,16,2048]{2,1,0:T(8,128)(2,1)S(1)} %get-tuple-element.8), channel_id=1, source_target_pairs={{1,0},{2,1},{3,2},{4,3},{5,4},{6,5},{7,6},{0,7},{9,8},{10,9},{11,1... | collective-permute-start | bytes 786440 | tf_op jit(solution)/shard_map/ppermute | solution.py:35
  36.0 0.0 copy-start
  36.0 3.6 %collective-permute-start.3 = (bf16[4,16,2048]{2,1,0:T(8,128)(2,1)S(1)}, bf16[4,16,2048]{2,1,0:T(8,128)(2,1)S(1)}, u32[]{:S(2)}, u32[]{:S(2)}) collective-permute-start(bf16[4,16,2048]{2,1,0:T(8,128)(2,1)S(1)} %get-tuple-element.7), channel_id=1, source_target_pairs={{7,0},{0,1},{1,2},{2,3},{3,4},{4,5},{5,6},{6,7},{15,8},{8,9},{9,10... | collective-permute-start | bytes 786440 | tf_op jit(solution)/shard_map/ppermute | solution.py:35
  39.7 3.9 %collective-permute-done = bf16[8,16,2048]{2,1,0:T(8,128)(2,1)S(1)} collective-permute-done((bf16[8,16,2048]{2,1,0:T(8,128)(2,1)S(1)}, bf16[8,16,2048]{2,1,0:T(8,128)(2,1)S(1)}, u32[]{:S(2)}, u32[]{:S(2)}) %collective-permute-start) | collective-permute-done | bytes 524320 | tf_op jit(solution)/shard_map/ppermute | solution.py:35
  43.6 4.2 %collective-permute-done.1 = bf16[8,16,2048]{2,1,0:T(8,128)(2,1)S(1)} collective-permute-done((bf16[8,16,2048]{2,1,0:T(8,128)(2,1)S(1)}, bf16[8,16,2048]{2,1,0:T(8,128)(2,1)S(1)}, u32[]{:S(2)}, u32[]{:S(2)}) %collective-permute-start.1) | collective-permute-done | bytes 524320 | tf_op jit(solution)/shard_map/ppermute | solution.py:35
  47.8 0.0 collective-permute-done.2
  47.9 0.0 collective-permute-done.3
  47.9 0.0 copy-done
  47.9 2.3 %fusion = f32[4,2,64,896]{3,2,1,0:T(8,128)S(1)} fusion(bf16[4,2,64,2048]{3,2,1,0:T(8,128)(2,1)S(1)} %bitcast.20, bf16[1,2048,896]{2,1,0:T(8,128)(2,1)S(1)} %copy-done), kind=kOutput, calls=%fused_computation | convolution fusion | flops 1879048192 | bytes 7602176 | tf_op jit(solution)/shard_map/dot_general | solution.py:97
  50.2 0.1 select_bitcast_fusion
  50.4 3.6 %collective-permute-start.4 = (f32[4,64,896]{2,1,0:T(8,128)S(1)}, f32[4,64,896]{2,1,0:T(8,128)S(1)}, u32[]{:S(2)}, u32[]{:S(2)}) collective-permute-start(f32[4,64,896]{2,1,0:T(8,128)S(1)} %get-tuple-element.5), channel_id=1, source_target_pairs={{0,32},{32,0},{64,96},{96,64},{128,160},{160,128},{192,224},{224,1... | collective-permute-start | bytes 2752520 | tf_op jit(solution)/shard_map/ppermute | solution.py:99
  54.0 2.1 %collective-permute-done.4 = f32[4,64,896]{2,1,0:T(8,128)S(1)} collective-permute-done((f32[4,64,896]{2,1,0:T(8,128)S(1)}, f32[4,64,896]{2,1,0:T(8,128)S(1)}, u32[]{:S(2)}, u32[]{:S(2)}) %collective-permute-start.4) | collective-permute-done | bytes 917536 | tf_op jit(solution)/shard_map/ppermute | solution.py:99
  56.1 0.3 pack.1
  56.4 25.7 %all_to_all.10.in_ref = s16[8,240,128]{2,1,0:T(8,128)(2,1)S(1)} all-to-all(s16[8,240,128]{2,1,0:T(8,128)(2,1)S(1)} %pack.1), channel_id=1, replica_groups={{0,64,128,192,256,320,384,448},{257,321,385,449,1,65,129,193},{2,66,130..., dimensions={0} | all-to-all | bytes 983040 | tf_op jit(solution)/shard_map/all_to_all | solution.py:111
  82.2 0.8 unpack_sum.1
  (7 shorter events, 0.2 us)
Async XLA Ops:
  2.4 26.3 %all-to-all-start = ((bf16[8,16,2048]{2,1,0:T(8,128)(2,1)}), bf16[8,16,2048]{2,1,0:T(8,128)(2,1)S(1)}, u32[]{:S(2)}, u32[]{:S(2)}) async-start(bf16[8,16,2048]{2,1,0:T(8,128)(2,1)} %broadcast_in_dim.14), calls=%async_computation | async-start | bytes 1048576 | tf_op jit(solution)/shard_map/all_to_all | solution.py:88
  28.6 14.9 %collective-permute-start = (bf16[8,16,2048]{2,1,0:T(8,128)(2,1)S(1)}, bf16[8,16,2048]{2,1,0:T(8,128)(2,1)S(1)}, u32[]{:S(2)}, u32[]{:S(2)}) collective-permute-start(bf16[8,16,2048]{2,1,0:T(8,128)(2,1)S(1)} %all-to-all-done), channel_id=1, source_target_pairs={{8,0},{9,1},{10,2},{11,3},{12,4},{13,5},{14,6},{15,7},{16,8},{17,9... | collective-permute-start | bytes 1572872 | tf_op jit(solution)/shard_map/ppermute | solution.py:35
  32.1 15.7 %collective-permute-start.1 = (bf16[8,16,2048]{2,1,0:T(8,128)(2,1)S(1)}, bf16[8,16,2048]{2,1,0:T(8,128)(2,1)S(1)}, u32[]{:S(2)}, u32[]{:S(2)}) collective-permute-start(bf16[8,16,2048]{2,1,0:T(8,128)(2,1)S(1)} %all-to-all-done), channel_id=1, source_target_pairs={{24,0},{25,1},{26,2},{27,3},{28,4},{29,5},{30,6},{31,7},{0,8},{1,9... | collective-permute-start | bytes 1572872 | tf_op jit(solution)/shard_map/ppermute | solution.py:35
  34.0 13.8 %collective-permute-start.2 = (bf16[4,16,2048]{2,1,0:T(8,128)(2,1)S(1)}, bf16[4,16,2048]{2,1,0:T(8,128)(2,1)S(1)}, u32[]{:S(2)}, u32[]{:S(2)}) collective-permute-start(bf16[4,16,2048]{2,1,0:T(8,128)(2,1)S(1)} %get-tuple-element.8), channel_id=1, source_target_pairs={{1,0},{2,1},{3,2},{4,3},{5,4},{6,5},{7,6},{0,7},{9,8},{10,9},{11,1... | collective-permute-start | bytes 786440 | tf_op jit(solution)/shard_map/ppermute | solution.py:35
  36.0 11.9 %copy-start = (bf16[1,2048,896]{2,1,0:T(8,128)(2,1)S(1)}, bf16[1,2048,896]{2,1,0:T(8,128)(2,1)}, u32[]{:S(2)}) copy-start(bf16[1,2048,896]{2,1,0:T(8,128)(2,1)} %param.4) | copy-start | bytes 11010052
  36.0 11.9 %collective-permute-start.3 = (bf16[4,16,2048]{2,1,0:T(8,128)(2,1)S(1)}, bf16[4,16,2048]{2,1,0:T(8,128)(2,1)S(1)}, u32[]{:S(2)}, u32[]{:S(2)}) collective-permute-start(bf16[4,16,2048]{2,1,0:T(8,128)(2,1)S(1)} %get-tuple-element.7), channel_id=1, source_target_pairs={{7,0},{0,1},{1,2},{2,3},{3,4},{4,5},{5,6},{6,7},{15,8},{8,9},{9,10... | collective-permute-start | bytes 786440 | tf_op jit(solution)/shard_map/ppermute | solution.py:35
  50.4 5.7 %collective-permute-start.4 = (f32[4,64,896]{2,1,0:T(8,128)S(1)}, f32[4,64,896]{2,1,0:T(8,128)S(1)}, u32[]{:S(2)}, u32[]{:S(2)}) collective-permute-start(f32[4,64,896]{2,1,0:T(8,128)S(1)} %get-tuple-element.5), channel_id=1, source_target_pairs={{0,32},{32,0},{64,96},{96,64},{128,160},{160,128},{192,224},{224,1... | collective-permute-start | bytes 2752520 | tf_op jit(solution)/shard_map/ppermute | solution.py:99

commit v4 on v3

--- a/solution.py
+++ b/solution.py
@@ -1,3 +1,5 @@
+import functools
+
 import jax
 import jax.numpy as jnp
 from jax import lax
@@ -35,17 +37,58 @@
     return lax.ppermute(block, "tr", pairs)
 
 
-def pack(ours_ref, given_ref, out_ref):
+def multiply(blocks, integrals_ref):
+    left = jnp.concatenate([block.reshape(-1, block.shape[-1]) for block in blocks], axis=0)
+    return jnp.dot(left, integrals_ref[0], preferred_element_type=jnp.float32)
+
+
+def this_core():
+    return lax.rem(lax.axis_index("grp"), 2)
+
+
+def near_product(own_ref, right_ref, integrals_ref, ours_ref, theirs_ref):
+    core = this_core()
+    count = ours_ref.shape[1]
+    own, right = own_ref[...], right_ref[...]
+    product = multiply([own, right], integrals_ref)
+    for d in range(2):
+        for k in range(2):
+            rows = product[(2 * d + k) * count : (2 * d + k + 1) * count]
+
+            @pl.when(core == k)
+            def _():
+                ours_ref[d] = rows
+
+            @pl.when(core != k)
+            def _():
+                theirs_ref[d] = rows
+
+
+def far_product(side, left_ref, up_ref, down_ref, integrals_ref, out_ref):
+    core = lax.rem(this_core() + side, 2)
+    half = up_ref.shape[0]
+    left = left_ref[pl.ds(core * half, half)]
+    across = jnp.where(core == 0, up_ref[...], down_ref[...])
+    product = multiply([left, across], integrals_ref)
+    count = out_ref.shape[1]
+    out_ref[0] = product[:count]
+    out_ref[1] = product[count:]
+
+
+def pack(near_ours_ref, near_given_ref, far_ours_ref, far_given_ref, out_ref):
     lanes = out_ref.shape[2]
-    rows = ours_ref.shape[3]
-    groups = ours_ref.shape[4] // lanes
-    slot = (0, 1, 3, 2)
+    rows = near_ours_ref.shape[1] // 4
+    groups = near_ours_ref.shape[2] // lanes
+    halves = ((near_ours_ref, near_given_ref), (far_ours_ref, far_given_ref))
+    place = ((0, 0), (0, 1), (1, 1), (1, 0))
     for d in range(CLASSES):
         for h in range(2):
             exponents = []
             for b in range(2):
-                at = (slot[(d + 2 * b) % CLASSES], h, b)
-                value = ours_ref[at] + given_ref[at]
+                which, at = place[(d + 2 * b) % CLASSES]
+                ours_ref, given_ref = halves[which]
+                span = pl.ds((2 * h + b) * rows, rows)
+                value = ours_ref[at, span, :] + given_ref[at, span, :]
                 top = jnp.max(jnp.abs(value), axis=1, keepdims=True)
                 exponent = jnp.ceil(jnp.log2(jnp.maximum(top, 2.0**-100)))
                 scaled = jnp.clip(jnp.round(value * jnp.exp2(15.0 - exponent)), -32767.0, 32767.0)
@@ -77,6 +120,26 @@
 
 
 LANES = 128
+LIMIT_DOT = 8
+
+
+def call(kernel, shapes, name, limit, flops=0):
+    vmem = pl.BlockSpec(memory_space=pltpu.VMEM)
+    single = not isinstance(shapes, tuple)
+
+    def run(*operands):
+        moved = sum(x.size * x.dtype.itemsize for x in (*operands, *((shapes,) if single else shapes)))
+        return pl.pallas_call(
+            kernel,
+            out_shape=shapes,
+            in_specs=[vmem] * len(operands),
+            out_specs=vmem if single else (vmem,) * len(shapes),
+            compiler_params=pltpu.CompilerParams(vmem_limit_bytes=limit << 20),
+            cost_estimate=pl.CostEstimate(flops=flops, bytes_accessed=moved, transcendentals=0),
+            name=name,
+        )(*operands)
+
+    return run
 
 
 def on_device(amplitudes, integrals, slab_count):
@@ -90,33 +153,19 @@
     left = from_neighbour(own, -1, 0)
     up = from_neighbour(own[:4], 0, 1)
     down = from_neighbour(own[4:], 0, -1)
-    mine = lax.rem(lax.axis_index("grp"), 2)
 
-    core0 = mine == 0
-    whole = jnp.concatenate([own, right, left, up, down], axis=0).reshape(-1, depth)
-    partial = jnp.dot(whole, integrals[0], preferred_element_type=jnp.float32)
-    partial = partial.reshape(CLASSES, 2, 4 * rows, width)
-    given = lax.ppermute(jnp.where(core0, partial[:, 1], partial[:, 0]), "grp", [(g, g ^ 1) for g in range(2 * Z)])
-    ours = jnp.where(core0, partial[:, 0], partial[:, 1])
-    shape = (CLASSES, 2, 2, rows, width)
-    vmem = pl.BlockSpec(memory_space=pltpu.VMEM)
-    packed = pl.pallas_call(
-        pack,
-        out_shape=jax.ShapeDtypeStruct((Z, 2 * rows * (width // LANES) + rows, LANES), jnp.int16),
-        in_specs=[vmem, vmem],
-        out_specs=vmem,
-        compiler_params=pltpu.CompilerParams(vmem_limit_bytes=4 << 20),
-        name="pack",
-    )(ours.reshape(shape), given.reshape(shape))
+    side = jax.ShapeDtypeStruct((2, 4 * rows, width), jnp.float32)
+    work = 2 * 8 * rows * depth * width
+    swap = [(g, g ^ 1) for g in range(2 * Z)]
+    near, near_theirs = call(near_product, (side, side), "near", LIMIT_DOT, 2 * work)(own, right, integrals)
+    near_given = lax.ppermute(near_theirs, "grp", swap)
+    far_theirs = call(functools.partial(far_product, 1), side, "far_theirs", LIMIT_DOT, work)(left, up, down, integrals)
+    far_given = lax.ppermute(far_theirs, "grp", swap)
+    far = call(functools.partial(far_product, 0), side, "far_ours", LIMIT_DOT, work)(left, up, down, integrals)
+    block = jax.ShapeDtypeStruct((Z, 2 * rows * (width // LANES) + rows, LANES), jnp.int16)
+    packed = call(pack, block, "pack", 4)(near, near_given, far, far_given)
     arrived = lax.all_to_all(packed, ("grp", "tr"), 0, 0, axis_index_groups=Z_GROUPS)
-    ladder = pl.pallas_call(
-        unpack_sum,
-        out_shape=jax.ShapeDtypeStruct((2 * rows, width), jnp.bfloat16),
-        in_specs=[vmem],
-        out_specs=vmem,
-        compiler_params=pltpu.CompilerParams(vmem_limit_bytes=2 << 20),
-        name="unpack_sum",
-    )(arrived)
+    ladder = call(unpack_sum, jax.ShapeDtypeStruct((2 * rows, width), jnp.bfloat16), "unpack_sum", 2)(arrived)
     return ladder[:, None, :]
 
 

time: 83.3 us -> 81.4 us (0.977)
  blocking collectives: 25.7 us -> 52.4 us
  waiting for transfers between devices: 27.1 us -> 3.88 us
  starting transfers between devices: 23.8 us -> 17.1 us
  Pallas kernels: 1.07 us -> 3.81 us
  matrix products: 2.33 us -> 0 us
  local copies, waits for them, and re-layouts: 1.04 us -> 2.13 us
    all_to_all x0 -> x1, blocking collectives: none -> 25.4 us  [on_device(): own = lax.all_to_all(copies, 'tr', 0, 0, axis_index_groups=CLASS_GROUPS)]
    all_to_all x1 -> x0, waiting for transfers between devices: 16.9 us -> none  [on_device(): own = lax.all_to_all(copies, 'tr', 0, 0, axis_index_groups=CLASS_GROUPS)]
    all_to_all x1 -> x0, starting transfers between devices: 9.33 us -> none  [on_device(): own = lax.all_to_all(copies, 'tr', 0, 0, axis_index_groups=CLASS_GROUPS)]
    ppermute x4, waiting for transfers between devices: 8.08 us -> 2.83 us  [from_neighbour(): return lax.ppermute(block, 'tr', pairs)]
    pallas_call x2 -> x5, Pallas kernels: 1.07 us -> 3.81 us  [run(): pl.pallas_call(kernel, out_shape=shapes, in_specs=[vmem] * len(operands),...]
    ppermute x1 -> x2, starting transfers between devices: 3.64 us -> 6.37 us  [the longest x1 4.45 us: on_device(): near_given = lax.ppermute(near_theirs, 'grp', swap)]
    dot_general x1 -> x0, matrix products: 2.33 us -> none  [on_device(): partial = jnp.dot(whole, integrals[0], preferred_element_type=jnp.float32)]
    unnamed x6 -> x4, local copies, waits for them, and re-layouts: 0.13 us -> 2.04 us
  transfers between devices with their start and end apart: 6 -> 6, of which waited for: 4 -> 2; matrix products, arithmetic and copies ran while one was open for 0% -> 0% of each run, Pallas kernels for 0% -> 3%
where the time goes in v4:
time: 81.4 us; the launch traced here: 81 us
  blocking collectives  52.4 us (64%)
  starting transfers between devices  17.1 us (21%)
  waiting for transfers between devices  3.88 us (5%)
  Pallas kernels  3.81 us (5%)
  local copies, waits for them, and re-layouts  2.13 us (3%)
  other arithmetic  0.86 us (1%)
    all_to_all x1, blocking collectives, on_device(): lax.all_to_all(packed, ('grp', 'tr'), 0, 0, axis_index_groups=Z_GROUPS)  27 us
    all_to_all x1, blocking collectives, on_device(): own = lax.all_to_all(copies, 'tr', 0, 0, axis_index_groups=CLASS_GROUPS)  25.4 us
    ppermute x4, starting transfers between devices, from_neighbour(): return lax.ppermute(block, 'tr', pairs)  10.8 us
    ppermute x1, starting transfers between devices, on_device(): near_given = lax.ppermute(near_theirs, 'grp', swap)  4.45 us
    pallas_call x5, Pallas kernels, run(): pl.pallas_call(kernel, out_shape=shapes, in_specs=[vmem] * len(operands),...  3.81 us
    ppermute x4, waiting for transfers between devices, from_neighbour(): return lax.ppermute(block, 'tr', pairs)  2.83 us
    unnamed x4, local copies, waits for them, and re-layouts  2.04 us
    ppermute x1, starting transfers between devices, on_device(): far_given = lax.ppermute(far_theirs, 'grp', swap)  1.92 us
  transfers between devices with their start and end apart: 6, of which 2 were waited for; matrix products, arithmetic and copies ran while one was open for 0% of the time, Pallas kernels for 3%

profile of v4, /device:TPU:1, one launch (start us, length us, event | category | flops | bytes accessed | tf_op | source)
XLA Modules:
  0.0 81.0 jit_solution(14779990528797326307)
XLA Ops:
  0.7 0.9 %bitcast_select_fusion = bf16[16,2048]{1,0:T(8,128)(2,1)S(1)} fusion(bf16[16,1,2048]{2,0,1:T(8,128)(2,1)} %param.3, pred[2048]{0:T(1024)(128)(4,1)S(1)} %iota_compare_fusion), kind=kLoop, calls=%fused_computation | loop fusion | flops 32768 | bytes 133120 | tf_op jit(solution)/shard_map/jit(_where)/select_n | solution.py:149
  1.6 25.4 %all_to_all.10.own_ref = bf16[8,16,2048]{2,1,0:T(8,128)(2,1)S(1)} all-to-all(bf16[8,16,2048]{2,1,0:T(8,128)(2,1)S(1)} %broadcast_in_dim.14), channel_id=1, replica_groups={{0,17,4,21,2,19,6,23},{8,25,12,29,10,27,14,31},{16,1,20,5,18,3,22,7},{2..., dimensions={0} | all-to-all | bytes 1048576 | tf_op jit(solution)/shard_map/all_to_all | solution.py:151
  27.0 3.6 %collective-permute-start = (bf16[8,16,2048]{2,1,0:T(8,128)(2,1)S(1)}, bf16[8,16,2048]{2,1,0:T(8,128)(2,1)S(1)}, u32[]{:S(2)}, u32[]{:S(2)}) collective-permute-start(bf16[8,16,2048]{2,1,0:T(8,128)(2,1)S(1)} %all_to_all.10.own_ref), channel_id=1, source_target_pairs={{8,0},{9,1},{10,2},{11,3},{12,4},{13,5},{14,6},{15,7},{16,8},{17,9... | collective-permute-start | bytes 1572872 | tf_op jit(solution)/shard_map/ppermute | solution.py:37
  30.6 1.9 %collective-permute-start.2 = (bf16[8,16,2048]{2,1,0:T(8,128)(2,1)S(1)}, bf16[8,16,2048]{2,1,0:T(8,128)(2,1)S(1)}, u32[]{:S(2)}, u32[]{:S(2)}) collective-permute-start(bf16[8,16,2048]{2,1,0:T(8,128)(2,1)S(1)} %all_to_all.10.own_ref), channel_id=1, source_target_pairs={{24,0},{25,1},{26,2},{27,3},{28,4},{29,5},{30,6},{31,7},{0,8},{1,9... | collective-permute-start | bytes 1572872 | tf_op jit(solution)/shard_map/ppermute | solution.py:37
  32.5 1.9 %collective-permute-start.3 = (bf16[4,16,2048]{2,1,0:T(8,128)(2,1)S(1)}, bf16[4,16,2048]{2,1,0:T(8,128)(2,1)S(1)}, u32[]{:S(2)}, u32[]{:S(2)}) collective-permute-start(bf16[4,16,2048]{2,1,0:T(8,128)(2,1)S(1)} %get-tuple-element.10), channel_id=1, source_target_pairs={{1,0},{2,1},{3,2},{4,3},{5,4},{6,5},{7,6},{0,7},{9,8},{10,9},{11,1... | collective-permute-start | bytes 786440 | tf_op jit(solution)/shard_map/ppermute | solution.py:37
  34.5 3.4 %collective-permute-start.4 = (bf16[4,16,2048]{2,1,0:T(8,128)(2,1)S(1)}, bf16[4,16,2048]{2,1,0:T(8,128)(2,1)S(1)}, u32[]{:S(2)}, u32[]{:S(2)}) collective-permute-start(bf16[4,16,2048]{2,1,0:T(8,128)(2,1)S(1)} %get-tuple-element.9), channel_id=1, source_target_pairs={{7,0},{0,1},{1,2},{2,3},{3,4},{4,5},{5,6},{6,7},{15,8},{8,9},{9,10... | collective-permute-start | bytes 786440 | tf_op jit(solution)/shard_map/ppermute | solution.py:37
  37.8 2.8 %collective-permute-done.right_ref = bf16[8,16,2048]{2,1,0:T(8,128)(2,1)S(1)} collective-permute-done((bf16[8,16,2048]{2,1,0:T(8,128)(2,1)S(1)}, bf16[8,16,2048]{2,1,0:T(8,128)(2,1)S(1)}, u32[]{:S(2)}, u32[]{:S(2)}) %collective-permute-start) | collective-permute-done | bytes 524320 | tf_op jit(solution)/shard_map/ppermute | solution.py:37
  40.7 0.0 copy-start
  40.7 2.0 %copy-done = bf16[1,2048,896]{2,1,0:T(8,128)(2,1)S(1)} copy-done((bf16[1,2048,896]{2,1,0:T(8,128)(2,1)S(1)}, bf16[1,2048,896]{2,1,0:T(8,128)(2,1)}, u32[]{:S(2)}) %copy-start) | copy-done | bytes 3670040
  42.7 0.0 copy-start.1
  42.7 1.3 %near.1 = (f32[2,64,896]{2,1,0:T(8,128)S(1)}, f32[2,64,896]{2,1,0:T(8,128)S(1)}) custom-call(bf16[8,16,2048]{2,1,0:T(8,128)(2,1)S(1)} %all_to_all.10.own_ref, bf16[8,16,2048]{2,1,0:T(8,128)(2,1)S(1)} %collective-permute-done.right_ref, bf16[1,2048,896]{2,1,0:T(8,128)(2,1)S(1)} %copy-done), custom_call_target="tpu_custom_call" | custom-call | flops 939524096 | bytes 5636096 | tf_op jit(solution)/shard_map/near/pallas_call | solution.py:132
  44.0 4.4 %collective-permute-start.1 = (f32[2,64,896]{2,1,0:T(8,128)S(1)}, f32[2,64,896]{2,1,0:T(8,128)S(1)}, u32[]{:S(2)}, u32[]{:S(2)}) collective-permute-start(f32[2,64,896]{2,1,0:T(8,128)S(1)} %get-tuple-element.8), channel_id=1, source_target_pairs={{0,32},{32,0},{64,96},{96,64},{128,160},{160,128},{192,224},{224,1... | collective-permute-start | bytes 1376264 | tf_op jit(solution)/shard_map/ppermute | solution.py:161
  48.5 0.0 collective-permute-done.3.up_ref
  48.5 0.0 collective-permute-done.4.down_ref
  48.5 0.0 collective-permute-done.2.left_ref
  48.5 0.0 copy-done.1
  48.5 0.7 far_theirs.1
  49.3 1.9 %collective-permute-start.5 = (f32[2,64,896]{2,1,0:T(8,128)S(1)}, f32[2,64,896]{2,1,0:T(8,128)S(1)}, u32[]{:S(2)}, u32[]{:S(2)}) collective-permute-start(f32[2,64,896]{2,1,0:T(8,128)S(1)} %far_theirs.1), channel_id=1, source_target_pairs={{0,32},{32,0},{64,96},{96,64},{128,160},{160,128},{192,224},{224,1... | collective-permute-start | bytes 1376264 | tf_op jit(solution)/shard_map/ppermute | solution.py:163
  51.2 0.7 far_ours.1.far_ours_ref
  51.9 0.0 collective-permute-done.1.near_given_ref
  51.9 1.0 %collective-permute-done.5.far_given_ref = f32[2,64,896]{2,1,0:T(8,128)S(1)} collective-permute-done((f32[2,64,896]{2,1,0:T(8,128)S(1)}, f32[2,64,896]{2,1,0:T(8,128)S(1)}, u32[]{:S(2)}, u32[]{:S(2)}) %collective-permute-start.5) | collective-permute-done | bytes 458784 | tf_op jit(solution)/shard_map/ppermute | solution.py:163
  53.0 0.3 pack.1
  53.2 27.0 %all_to_all.11.in_ref = s16[8,240,128]{2,1,0:T(8,128)(2,1)S(1)} all-to-all(s16[8,240,128]{2,1,0:T(8,128)(2,1)S(1)} %pack.1), channel_id=1, replica_groups={{0,64,128,192,256,320,384,448},{257,321,385,449,1,65,129,193},{2,66,130..., dimensions={0} | all-to-all | bytes 983040 | tf_op jit(solution)/shard_map/all_to_all | solution.py:167
  80.3 0.8 unpack_sum.1
  (3 shorter events, 0.1 us)
Async XLA Ops:
  27.0 13.7 %collective-permute-start = (bf16[8,16,2048]{2,1,0:T(8,128)(2,1)S(1)}, bf16[8,16,2048]{2,1,0:T(8,128)(2,1)S(1)}, u32[]{:S(2)}, u32[]{:S(2)}) collective-permute-start(bf16[8,16,2048]{2,1,0:T(8,128)(2,1)S(1)} %all_to_all.10.own_ref), channel_id=1, source_target_pairs={{8,0},{9,1},{10,2},{11,3},{12,4},{13,5},{14,6},{15,7},{16,8},{17,9... | collective-permute-start | bytes 1572872 | tf_op jit(solution)/shard_map/ppermute | solution.py:37
  30.6 17.9 %collective-permute-start.2 = (bf16[8,16,2048]{2,1,0:T(8,128)(2,1)S(1)}, bf16[8,16,2048]{2,1,0:T(8,128)(2,1)S(1)}, u32[]{:S(2)}, u32[]{:S(2)}) collective-permute-start(bf16[8,16,2048]{2,1,0:T(8,128)(2,1)S(1)} %all_to_all.10.own_ref), channel_id=1, source_target_pairs={{24,0},{25,1},{26,2},{27,3},{28,4},{29,5},{30,6},{31,7},{0,8},{1,9... | collective-permute-start | bytes 1572872 | tf_op jit(solution)/shard_map/ppermute | solution.py:37
  32.5 15.9 %collective-permute-start.3 = (bf16[4,16,2048]{2,1,0:T(8,128)(2,1)S(1)}, bf16[4,16,2048]{2,1,0:T(8,128)(2,1)S(1)}, u32[]{:S(2)}, u32[]{:S(2)}) collective-permute-start(bf16[4,16,2048]{2,1,0:T(8,128)(2,1)S(1)} %get-tuple-element.10), channel_id=1, source_target_pairs={{1,0},{2,1},{3,2},{4,3},{5,4},{6,5},{7,6},{0,7},{9,8},{10,9},{11,1... | collective-permute-start | bytes 786440 | tf_op jit(solution)/shard_map/ppermute | solution.py:37
  34.5 14.0 %collective-permute-start.4 = (bf16[4,16,2048]{2,1,0:T(8,128)(2,1)S(1)}, bf16[4,16,2048]{2,1,0:T(8,128)(2,1)S(1)}, u32[]{:S(2)}, u32[]{:S(2)}) collective-permute-start(bf16[4,16,2048]{2,1,0:T(8,128)(2,1)S(1)} %get-tuple-element.9), channel_id=1, source_target_pairs={{7,0},{0,1},{1,2},{2,3},{3,4},{4,5},{5,6},{6,7},{15,8},{8,9},{9,10... | collective-permute-start | bytes 786440 | tf_op jit(solution)/shard_map/ppermute | solution.py:37
  40.7 2.0 %copy-start = (bf16[1,2048,896]{2,1,0:T(8,128)(2,1)S(1)}, bf16[1,2048,896]{2,1,0:T(8,128)(2,1)}, u32[]{:S(2)}) copy-start(bf16[1,2048,896]{2,1,0:T(8,128)(2,1)} %integrals_ref.5) | copy-start | bytes 11010052
  42.7 5.8 %copy-start.1 = (bf16[1,2048,896]{2,1,0:T(8,128)(2,1)S(1)}, bf16[1,2048,896]{2,1,0:T(8,128)(2,1)}, u32[]{:S(2)}) copy-start(bf16[1,2048,896]{2,1,0:T(8,128)(2,1)} %integrals_ref.5) | copy-start | bytes 11010052
  44.0 7.9 %collective-permute-start.1 = (f32[2,64,896]{2,1,0:T(8,128)S(1)}, f32[2,64,896]{2,1,0:T(8,128)S(1)}, u32[]{:S(2)}, u32[]{:S(2)}) collective-permute-start(f32[2,64,896]{2,1,0:T(8,128)S(1)} %get-tuple-element.8), channel_id=1, source_target_pairs={{0,32},{32,0},{64,96},{96,64},{128,160},{160,128},{192,224},{224,1... | collective-permute-start | bytes 1376264 | tf_op jit(solution)/shard_map/ppermute | solution.py:161
  49.3 3.7 %collective-permute-start.5 = (f32[2,64,896]{2,1,0:T(8,128)S(1)}, f32[2,64,896]{2,1,0:T(8,128)S(1)}, u32[]{:S(2)}, u32[]{:S(2)}) collective-permute-start(f32[2,64,896]{2,1,0:T(8,128)S(1)} %far_theirs.1), channel_id=1, source_target_pairs={{0,32},{32,0},{64,96},{96,64},{128,160},{160,128},{192,224},{224,1... | collective-permute-start | bytes 1376264 | tf_op jit(solution)/shard_map/ppermute | solution.py:163

commit v5 on v4

--- a/solution.py
+++ b/solution.py
@@ -44,6 +44,11 @@
 
 def this_core():
     return lax.rem(lax.axis_index("grp"), 2)
+
+
+def split(own_ref, low_ref, high_ref):
+    low_ref[...] = own_ref[:4]
+    high_ref[...] = own_ref[4:]
 
 
 def near_product(own_ref, right_ref, integrals_ref, ours_ref, theirs_ref):
@@ -151,8 +156,10 @@
     own = lax.all_to_all(copies, "tr", 0, 0, axis_index_groups=CLASS_GROUPS)
     right = from_neighbour(own, 1, 0)
     left = from_neighbour(own, -1, 0)
-    up = from_neighbour(own[:4], 0, 1)
-    down = from_neighbour(own[4:], 0, -1)
+    half = jax.ShapeDtypeStruct((4, rows, depth), own.dtype)
+    low, high = call(split, (half, half), "split", 4, 4000000000)(own)
+    up = from_neighbour(low, 0, 1)
+    down = from_neighbour(high, 0, -1)
 
     side = jax.ShapeDtypeStruct((2, 4 * rows, width), jnp.float32)
     work = 2 * 8 * rows * depth * width

time: 81.4 us -> 79.8 us (0.980)
  local copies, waits for them, and re-layouts: 2.13 us -> 0.05 us
  starting transfers between devices: 17.1 us -> 18.9 us
  blocking collectives: 52.4 us -> 51.2 us
    unnamed x4 -> x2, local copies, waits for them, and re-layouts: 2.04 us -> 0.01 us
    ppermute x1, starting transfers between devices: 1.92 us -> 3.43 us  [on_device(): far_given = lax.ppermute(far_theirs, 'grp', swap)]
    all_to_all x1, blocking collectives: 27 us -> 25.7 us  [on_device(): lax.all_to_all(packed, ('grp', 'tr'), 0, 0, axis_index_groups=Z_GROUPS)]
    pallas_call x5 -> x6, Pallas kernels: 3.81 us -> 3.84 us  [run(): pl.pallas_call(kernel, out_shape=shapes, in_specs=[vmem] * len(operands),...]
  transfers between devices with their start and end apart: 6 -> 6, of which waited for: 2 -> 2; matrix products, arithmetic and copies ran while one was open for 0% -> 0% of each run, Pallas kernels for 3% -> 4%
where the time goes in v5:
time: 79.8 us; the launch traced here: 79.1 us
  blocking collectives  51.2 us (64%)
  starting transfers between devices  18.9 us (24%)
  Pallas kernels  3.84 us (5%)
  waiting for transfers between devices  3.52 us (4%)
  other arithmetic  0.86 us (1%)
    all_to_all x1, blocking collectives, on_device(): lax.all_to_all(packed, ('grp', 'tr'), 0, 0, axis_index_groups=Z_GROUPS)  25.7 us
    all_to_all x1, blocking collectives, on_device(): own = lax.all_to_all(copies, 'tr', 0, 0, axis_index_groups=CLASS_GROUPS)  25.4 us
    ppermute x4, starting transfers between devices, from_neighbour(): return lax.ppermute(block, 'tr', pairs)  11 us
    ppermute x1, starting transfers between devices, on_device(): near_given = lax.ppermute(near_theirs, 'grp', swap)  4.45 us
    pallas_call x6, Pallas kernels, run(): pl.pallas_call(kernel, out_shape=shapes, in_specs=[vmem] * len(operands),...  3.84 us
    ppermute x1, starting transfers between devices, on_device(): far_given = lax.ppermute(far_theirs, 'grp', swap)  3.43 us
    ppermute x4, waiting for transfers between devices, from_neighbour(): return lax.ppermute(block, 'tr', pairs)  2.83 us
  transfers between devices with their start and end apart: 6, of which 2 were waited for; matrix products, arithmetic and copies ran while one was open for 0% of the time, Pallas kernels for 4%

profile of v5, /device:TPU:1, one launch (start us, length us, event | category | flops | bytes accessed | tf_op | source)
XLA Modules:
  0.0 79.1 jit_solution(4971038643773074799)
XLA Ops:
  0.7 0.9 %bitcast_select_fusion = bf16[16,2048]{1,0:T(8,128)(2,1)S(1)} fusion(bf16[16,1,2048]{2,0,1:T(8,128)(2,1)} %param.3, pred[2048]{0:T(1024)(128)(4,1)S(1)} %iota_compare_fusion), kind=kLoop, calls=%fused_computation | loop fusion | flops 32768 | bytes 133120 | tf_op jit(solution)/shard_map/jit(_where)/select_n | solution.py:154
  1.6 25.4 %all_to_all.10.own_ref = bf16[8,16,2048]{2,1,0:T(8,128)(2,1)S(1)} all-to-all(bf16[8,16,2048]{2,1,0:T(8,128)(2,1)S(1)} %broadcast_in_dim.14), channel_id=1, replica_groups={{0,17,4,21,2,19,6,23},{8,25,12,29,10,27,14,31},{16,1,20,5,18,3,22,7},{2..., dimensions={0} | all-to-all | bytes 1048576 | tf_op jit(solution)/shard_map/all_to_all | solution.py:156
  27.0 0.0 copy-start
  27.0 3.8 %collective-permute-start = (bf16[8,16,2048]{2,1,0:T(8,128)(2,1)S(1)}, bf16[8,16,2048]{2,1,0:T(8,128)(2,1)S(1)}, u32[]{:S(2)}, u32[]{:S(2)}) collective-permute-start(bf16[8,16,2048]{2,1,0:T(8,128)(2,1)S(1)} %all_to_all.10.own_ref), channel_id=1, source_target_pairs={{8,0},{9,1},{10,2},{11,3},{12,4},{13,5},{14,6},{15,7},{16,8},{17,9... | collective-permute-start | bytes 1572872 | tf_op jit(solution)/shard_map/ppermute | solution.py:37
  30.8 1.9 %collective-permute-start.2 = (bf16[8,16,2048]{2,1,0:T(8,128)(2,1)S(1)}, bf16[8,16,2048]{2,1,0:T(8,128)(2,1)S(1)}, u32[]{:S(2)}, u32[]{:S(2)}) collective-permute-start(bf16[8,16,2048]{2,1,0:T(8,128)(2,1)S(1)} %all_to_all.10.own_ref), channel_id=1, source_target_pairs={{24,0},{25,1},{26,2},{27,3},{28,4},{29,5},{30,6},{31,7},{0,8},{1,9... | collective-permute-start | bytes 1572872 | tf_op jit(solution)/shard_map/ppermute | solution.py:37
  32.8 1.9 %collective-permute-start.3 = (bf16[4,16,2048]{2,1,0:T(8,128)(2,1)S(1)}, bf16[4,16,2048]{2,1,0:T(8,128)(2,1)S(1)}, u32[]{:S(2)}, u32[]{:S(2)}) collective-permute-start(bf16[4,16,2048]{2,1,0:T(8,128)(2,1)S(1)} %get-tuple-element.11), channel_id=1, source_target_pairs={{1,0},{2,1},{3,2},{4,3},{5,4},{6,5},{7,6},{0,7},{9,8},{10,9},{11,1... | collective-permute-start | bytes 786440 | tf_op jit(solution)/shard_map/ppermute | solution.py:37
  34.7 3.4 %collective-permute-start.4 = (bf16[4,16,2048]{2,1,0:T(8,128)(2,1)S(1)}, bf16[4,16,2048]{2,1,0:T(8,128)(2,1)S(1)}, u32[]{:S(2)}, u32[]{:S(2)}) collective-permute-start(bf16[4,16,2048]{2,1,0:T(8,128)(2,1)S(1)} %get-tuple-element.12), channel_id=1, source_target_pairs={{7,0},{0,1},{1,2},{2,3},{3,4},{4,5},{5,6},{6,7},{15,8},{8,9},{9,10... | collective-permute-start | bytes 786440 | tf_op jit(solution)/shard_map/ppermute | solution.py:37
  38.1 2.8 %collective-permute-done.right_ref = bf16[8,16,2048]{2,1,0:T(8,128)(2,1)S(1)} collective-permute-done((bf16[8,16,2048]{2,1,0:T(8,128)(2,1)S(1)}, bf16[8,16,2048]{2,1,0:T(8,128)(2,1)S(1)}, u32[]{:S(2)}, u32[]{:S(2)}) %collective-permute-start) | collective-permute-done | bytes 524320 | tf_op jit(solution)/shard_map/ppermute | solution.py:37
  40.9 0.0 copy-done
  40.9 1.3 %near.1 = (f32[2,64,896]{2,1,0:T(8,128)S(1)}, f32[2,64,896]{2,1,0:T(8,128)S(1)}) custom-call(bf16[8,16,2048]{2,1,0:T(8,128)(2,1)S(1)} %all_to_all.10.own_ref, bf16[8,16,2048]{2,1,0:T(8,128)(2,1)S(1)} %collective-permute-done.right_ref, bf16[1,2048,896]{2,1,0:T(8,128)(2,1)S(1)} %copy-done), custom_call_target="tpu_custom_call" | custom-call | flops 939524096 | bytes 5636096 | tf_op jit(solution)/shard_map/near/pallas_call | solution.py:137
  42.3 4.4 %collective-permute-start.1 = (f32[2,64,896]{2,1,0:T(8,128)S(1)}, f32[2,64,896]{2,1,0:T(8,128)S(1)}, u32[]{:S(2)}, u32[]{:S(2)}) collective-permute-start(f32[2,64,896]{2,1,0:T(8,128)S(1)} %get-tuple-element.10), channel_id=1, source_target_pairs={{0,32},{32,0},{64,96},{96,64},{128,160},{160,128},{192,224},{224,1... | collective-permute-start | bytes 1376264 | tf_op jit(solution)/shard_map/ppermute | solution.py:168
  46.7 0.0 collective-permute-done.3.up_ref
  46.7 0.0 collective-permute-done.4.down_ref
  46.7 0.0 collective-permute-done.2.left_ref
  46.7 0.7 far_theirs.1
  47.5 3.4 %collective-permute-start.5 = (f32[2,64,896]{2,1,0:T(8,128)S(1)}, f32[2,64,896]{2,1,0:T(8,128)S(1)}, u32[]{:S(2)}, u32[]{:S(2)}) collective-permute-start(f32[2,64,896]{2,1,0:T(8,128)S(1)} %far_theirs.1), channel_id=1, source_target_pairs={{0,32},{32,0},{64,96},{96,64},{128,160},{160,128},{192,224},{224,1... | collective-permute-start | bytes 1376264 | tf_op jit(solution)/shard_map/ppermute | solution.py:170
  50.9 0.7 far_ours.1.far_ours_ref
  51.6 0.0 collective-permute-done.1.near_given_ref
  51.7 0.7 collective-permute-done.5.far_given_ref
  52.3 0.3 pack.1
  52.6 25.7 %all_to_all.11.in_ref = s16[8,240,128]{2,1,0:T(8,128)(2,1)S(1)} all-to-all(s16[8,240,128]{2,1,0:T(8,128)(2,1)S(1)} %pack.1), channel_id=1, replica_groups={{0,64,128,192,256,320,384,448},{257,321,385,449,1,65,129,193},{2,66,130..., dimensions={0} | all-to-all | bytes 983040 | tf_op jit(solution)/shard_map/all_to_all | solution.py:174
  78.4 0.8 unpack_sum.1
  (3 shorter events, 0.1 us)
Async XLA Ops:
  27.0 13.9 %copy-start = (bf16[1,2048,896]{2,1,0:T(8,128)(2,1)S(1)}, bf16[1,2048,896]{2,1,0:T(8,128)(2,1)}, u32[]{:S(2)}) copy-start(bf16[1,2048,896]{2,1,0:T(8,128)(2,1)} %integrals_ref.5) | copy-start | bytes 11010052
  27.0 13.9 %collective-permute-start = (bf16[8,16,2048]{2,1,0:T(8,128)(2,1)S(1)}, bf16[8,16,2048]{2,1,0:T(8,128)(2,1)S(1)}, u32[]{:S(2)}, u32[]{:S(2)}) collective-permute-start(bf16[8,16,2048]{2,1,0:T(8,128)(2,1)S(1)} %all_to_all.10.own_ref), channel_id=1, source_target_pairs={{8,0},{9,1},{10,2},{11,3},{12,4},{13,5},{14,6},{15,7},{16,8},{17,9... | collective-permute-start | bytes 1572872 | tf_op jit(solution)/shard_map/ppermute | solution.py:37
  30.8 15.9 %collective-permute-start.2 = (bf16[8,16,2048]{2,1,0:T(8,128)(2,1)S(1)}, bf16[8,16,2048]{2,1,0:T(8,128)(2,1)S(1)}, u32[]{:S(2)}, u32[]{:S(2)}) collective-permute-start(bf16[8,16,2048]{2,1,0:T(8,128)(2,1)S(1)} %all_to_all.10.own_ref), channel_id=1, source_target_pairs={{24,0},{25,1},{26,2},{27,3},{28,4},{29,5},{30,6},{31,7},{0,8},{1,9... | collective-permute-start | bytes 1572872 | tf_op jit(solution)/shard_map/ppermute | solution.py:37
  32.8 13.9 %collective-permute-start.3 = (bf16[4,16,2048]{2,1,0:T(8,128)(2,1)S(1)}, bf16[4,16,2048]{2,1,0:T(8,128)(2,1)S(1)}, u32[]{:S(2)}, u32[]{:S(2)}) collective-permute-start(bf16[4,16,2048]{2,1,0:T(8,128)(2,1)S(1)} %get-tuple-element.11), channel_id=1, source_target_pairs={{1,0},{2,1},{3,2},{4,3},{5,4},{6,5},{7,6},{0,7},{9,8},{10,9},{11,1... | collective-permute-start | bytes 786440 | tf_op jit(solution)/shard_map/ppermute | solution.py:37
  34.7 12.0 %collective-permute-start.4 = (bf16[4,16,2048]{2,1,0:T(8,128)(2,1)S(1)}, bf16[4,16,2048]{2,1,0:T(8,128)(2,1)S(1)}, u32[]{:S(2)}, u32[]{:S(2)}) collective-permute-start(bf16[4,16,2048]{2,1,0:T(8,128)(2,1)S(1)} %get-tuple-element.12), channel_id=1, source_target_pairs={{7,0},{0,1},{1,2},{2,3},{3,4},{4,5},{5,6},{6,7},{15,8},{8,9},{9,10... | collective-permute-start | bytes 786440 | tf_op jit(solution)/shard_map/ppermute | solution.py:37
  42.3 9.4 %collective-permute-start.1 = (f32[2,64,896]{2,1,0:T(8,128)S(1)}, f32[2,64,896]{2,1,0:T(8,128)S(1)}, u32[]{:S(2)}, u32[]{:S(2)}) collective-permute-start(f32[2,64,896]{2,1,0:T(8,128)S(1)} %get-tuple-element.10), channel_id=1, source_target_pairs={{0,32},{32,0},{64,96},{96,64},{128,160},{160,128},{192,224},{224,1... | collective-permute-start | bytes 1376264 | tf_op jit(solution)/shard_map/ppermute | solution.py:168
  47.5 4.9 %collective-permute-start.5 = (f32[2,64,896]{2,1,0:T(8,128)S(1)}, f32[2,64,896]{2,1,0:T(8,128)S(1)}, u32[]{:S(2)}, u32[]{:S(2)}) collective-permute-start(f32[2,64,896]{2,1,0:T(8,128)S(1)} %far_theirs.1), channel_id=1, source_target_pairs={{0,32},{32,0},{64,96},{96,64},{128,160},{160,128},{192,224},{224,1... | collective-permute-start | bytes 1376264 | tf_op jit(solution)/shard_map/ppermute | solution.py:170

commit v6 on v4

--- a/solution.py
+++ b/solution.py
@@ -15,8 +15,10 @@
     return (x % X) * Y + y % Y
 
 
-ORDER = [4 * h + 2 * k + b for k in range(2) for h in range(2) for b in range(2)]
+ORDER = (0, 2, 4, 6, 1, 3, 5, 7)
 CLASS_GROUPS = [[tr_of(c - 2 * y, y) for y in ORDER] for c in range(CLASSES)]
+
+FOLD = (0, 7, 1, 6, 2, 5, 3, 4)
 
 
 def z_groups():
@@ -24,16 +26,19 @@
     for core in range(2):
         for t in range(X * Y):
             c = (t // Y + 2 * (t % Y)) % CLASSES
-            planes = [2 * ((c + d) % X) + h for d in range(CLASSES) for h in range(2)]
-            groups.append([(2 * z + core) * X * Y + t for z in planes])
+            groups.append([(2 * ((2 * c + plane) % Z) + core) * X * Y + t for plane in FOLD])
     return groups
 
 
 Z_GROUPS = z_groups()
 
 
-def from_neighbour(block, dx, dy):
-    pairs = [(tr_of(t // Y + dx, t % Y + dy), t) for t in range(X * Y)]
+def exchange(block, dx, dy):
+    pairs = []
+    for t in range(X * Y):
+        x, y = t // Y, t % Y
+        sign = 1 - 2 * ((x if dx else y) % 2)
+        pairs.append((tr_of(x + sign * dx, y + sign * dy), t))
     return lax.ppermute(block, "tr", pairs)
 
 
@@ -46,30 +51,36 @@
     return lax.rem(lax.axis_index("grp"), 2)
 
 
+def split(own_ref, low_ref, high_ref):
+    low_ref[...] = own_ref[:MOST]
+    high_ref[...] = own_ref[MOST:]
+
+
 def near_product(own_ref, right_ref, integrals_ref, ours_ref, theirs_ref):
     core = this_core()
-    count = ours_ref.shape[1]
-    own, right = own_ref[...], right_ref[...]
-    product = multiply([own, right], integrals_ref)
+    rows = own_ref.shape[1]
+    product = multiply([own_ref[...], right_ref[...]], integrals_ref)
     for d in range(2):
-        for k in range(2):
-            rows = product[(2 * d + k) * count : (2 * d + k + 1) * count]
+        for block in range(8):
+            start = (8 * d + block) * rows
+            values = product[start : start + rows]
+            span = pl.ds(block // 2 * rows, rows)
 
-            @pl.when(core == k)
+            @pl.when(core == block % 2)
             def _():
-                ours_ref[d] = rows
+                ours_ref[d, span] = values
 
-            @pl.when(core != k)
+            @pl.when(core != block % 2)
             def _():
-                theirs_ref[d] = rows
+                theirs_ref[d, span] = values
 
 
 def far_product(side, left_ref, up_ref, down_ref, integrals_ref, out_ref):
     core = lax.rem(this_core() + side, 2)
-    half = up_ref.shape[0]
-    left = left_ref[pl.ds(core * half, half)]
-    across = jnp.where(core == 0, up_ref[...], down_ref[...])
-    product = multiply([left, across], integrals_ref)
+    blocks = [left_ref[core + 2 * i] for i in range(4)]
+    across = [up_ref[i] for i in range(MOST)] + [down_ref[i] for i in range(8 - MOST)]
+    blocks += [jnp.where(core == 0, across[2 * i], across[2 * i + 1]) for i in range(4)]
+    product = multiply(blocks, integrals_ref)
     count = out_ref.shape[1]
     out_ref[0] = product[:count]
     out_ref[1] = product[count:]
@@ -79,26 +90,32 @@
     lanes = out_ref.shape[2]
     rows = near_ours_ref.shape[1] // 4
     groups = near_ours_ref.shape[2] // lanes
-    halves = ((near_ours_ref, near_given_ref), (far_ours_ref, far_given_ref))
-    place = ((0, 0), (0, 1), (1, 1), (1, 0))
-    for d in range(CLASSES):
-        for h in range(2):
-            exponents = []
-            for b in range(2):
-                which, at = place[(d + 2 * b) % CLASSES]
-                ours_ref, given_ref = halves[which]
-                span = pl.ds((2 * h + b) * rows, rows)
-                value = ours_ref[at, span, :] + given_ref[at, span, :]
-                top = jnp.max(jnp.abs(value), axis=1, keepdims=True)
-                exponent = jnp.ceil(jnp.log2(jnp.maximum(top, 2.0**-100)))
-                scaled = jnp.clip(jnp.round(value * jnp.exp2(15.0 - exponent)), -32767.0, 32767.0)
-                number = scaled.astype(jnp.int32).astype(jnp.int16)
-                for g in range(groups):
-                    out_ref[2 * d + h, pl.ds((2 * g + b) * rows, rows), :] = number[:, g * lanes : (g + 1) * lanes]
-                exponents.append(jnp.broadcast_to(exponent, (rows, lanes)))
-            lower = lax.broadcasted_iota(jnp.int32, (rows, lanes), 1) < lanes // 2
-            both = jnp.where(lower, exponents[0], exponents[1])
-            out_ref[2 * d + h, pl.ds(2 * groups * rows, rows), :] = both.astype(jnp.int32).astype(jnp.int16)
+    ours = [near_ours_ref.at[0], near_ours_ref.at[1], far_ours_ref.at[1], far_ours_ref.at[0]]
+    given = [near_given_ref.at[0], near_given_ref.at[1], far_given_ref.at[1], far_given_ref.at[0]]
+    odd = lax.rem(lax.axis_index("tr") // Y, 2)
+    for way in range(2):
+
+        @pl.when(odd == way)
+        def _():
+            for d in range(CLASSES):
+                for h in range(2):
+                    place_out = FOLD.index(2 * d + h)
+                    exponents = []
+                    for b in range(2):
+                        at = (1 - 2 * way) * ((d + 2 * b) % CLASSES)
+                        span = pl.ds((2 * b + h) * rows, rows)
+                        value = ours[at][span, :] + given[at][span, :]
+                        top = jnp.max(jnp.abs(value), axis=1, keepdims=True)
+                        exponent = jnp.ceil(jnp.log2(jnp.maximum(top, 2.0**-100)))
+                        scaled = jnp.clip(jnp.round(value * jnp.exp2(15.0 - exponent)), -32767.0, 32767.0)
+                        number = scaled.astype(jnp.int32).astype(jnp.int16)
+                        for g in range(groups):
+                            lane = pl.ds((2 * g + b) * rows, rows)
+                            out_ref[place_out, lane, :] = number[:, g * lanes : (g + 1) * lanes]
+                        exponents.append(jnp.broadcast_to(exponent, (rows, lanes)))
+                    lower = lax.broadcasted_iota(jnp.int32, (rows, lanes), 1) < lanes // 2
+                    both = jnp.where(lower, exponents[0], exponents[1])
+                    out_ref[place_out, pl.ds(2 * groups * rows, rows), :] = both.astype(jnp.int32).astype(jnp.int16)
 
 
 def unpack_sum(in_ref, out_ref):
@@ -121,6 +138,7 @@
 
 LANES = 128
 LIMIT_DOT = 8
+MOST = 5
 
 
 def call(kernel, shapes, name, limit, flops=0):
@@ -149,10 +167,12 @@
     masked = jnp.where(column < slab_count[0, 0], amplitudes[:, 0, :], jnp.zeros((), amplitudes.dtype))
     copies = jnp.broadcast_to(masked[None], (8, rows, depth))
     own = lax.all_to_all(copies, "tr", 0, 0, axis_index_groups=CLASS_GROUPS)
-    right = from_neighbour(own, 1, 0)
-    left = from_neighbour(own, -1, 0)
-    up = from_neighbour(own[:4], 0, 1)
-    down = from_neighbour(own[4:], 0, -1)
+    right = exchange(own, 1, 0)
+    left = exchange(own, -1, 0)
+    parts = tuple(jax.ShapeDtypeStruct((n, rows, depth), own.dtype) for n in (MOST, 8 - MOST))
+    low, high = call(split, parts, "split", 4, 4000000000)(own)
+    up = exchange(low, 0, 1)
+    down = exchange(high, 0, -1)
 
     side = jax.ShapeDtypeStruct((2, 4 * rows, width), jnp.float32)
     work = 2 * 8 * rows * depth * width

time: 81.4 us -> 78.3 us (0.962)
  local copies, waits for them, and re-layouts: 2.13 us -> 0.05 us
  blocking collectives: 52.4 us -> 50.4 us
  starting transfers between devices: 17.1 us -> 19.1 us
  waiting for transfers between devices: 3.88 us -> 2.68 us
    unnamed x4 -> x2, local copies, waits for them, and re-layouts: 2.04 us -> 0.01 us
    all_to_all x1, blocking collectives: 27 us -> 25 us  [on_device(): lax.all_to_all(packed, ('grp', 'tr'), 0, 0, axis_index_groups=Z_GROUPS)]
    ppermute x4, starting transfers between devices: 10.8 us -> 12.1 us  [exchange(): return lax.ppermute(block, 'tr', pairs)]
    ppermute x4, waiting for transfers between devices: 2.83 us -> 1.99 us  [exchange(): return lax.ppermute(block, 'tr', pairs)]
    ppermute x1, starting transfers between devices: 1.92 us -> 2.75 us  [on_device(): far_given = lax.ppermute(far_theirs, 'grp', swap)]
    pallas_call x5 -> x6, Pallas kernels: 3.81 us -> 3.89 us  [run(): pl.pallas_call(kernel, out_shape=shapes, in_specs=[vmem] * len(operands),...]
  transfers between devices with their start and end apart: 6 -> 6, of which waited for: 2 -> 2; matrix products, arithmetic and copies ran while one was open for 0% -> 0% of each run, Pallas kernels for 3% -> 4%
where the time goes in v6:
time: 78.3 us; the launch traced here: 77.8 us
  blocking collectives  50.4 us (64%)
  starting transfers between devices  19.1 us (24%)
  Pallas kernels  3.89 us (5%)
  waiting for transfers between devices  2.68 us (3%)
  other arithmetic  0.86 us (1%)
  between operations  0.79 us (1%)
    all_to_all x1, blocking collectives, on_device(): own = lax.all_to_all(copies, 'tr', 0, 0, axis_index_groups=CLASS_GROUPS)  25.4 us
    all_to_all x1, blocking collectives, on_device(): lax.all_to_all(packed, ('grp', 'tr'), 0, 0, axis_index_groups=Z_GROUPS)  25 us
    ppermute x4, starting transfers between devices, exchange(): return lax.ppermute(block, 'tr', pairs)  12.1 us
    ppermute x1, starting transfers between devices, on_device(): near_given = lax.ppermute(near_theirs, 'grp', swap)  4.24 us
    pallas_call x6, Pallas kernels, run(): pl.pallas_call(kernel, out_shape=shapes, in_specs=[vmem] * len(operands),...  3.89 us
    ppermute x1, starting transfers between devices, on_device(): far_given = lax.ppermute(far_theirs, 'grp', swap)  2.75 us
    ppermute x4, waiting for transfers between devices, exchange(): return lax.ppermute(block, 'tr', pairs)  1.99 us
  transfers between devices with their start and end apart: 6, of which 2 were waited for; matrix products, arithmetic and copies ran while one was open for 0% of the time, Pallas kernels for 4%

profile of v6, /device:TPU:1, one launch (start us, length us, event | category | flops | bytes accessed | tf_op | source)
XLA Modules:
  0.0 77.8 jit_solution(9567600948997910999)
XLA Ops:
  0.7 0.9 %bitcast_select_fusion = bf16[16,2048]{1,0:T(8,128)(2,1)S(1)} fusion(bf16[16,1,2048]{2,0,1:T(8,128)(2,1)} %param.3, pred[2048]{0:T(1024)(128)(4,1)S(1)} %iota_compare_fusion), kind=kLoop, calls=%fused_computation | loop fusion | flops 32768 | bytes 133120 | tf_op jit(solution)/shard_map/jit(_where)/select_n | solution.py:167
  1.6 25.4 %all_to_all.10.own_ref = bf16[8,16,2048]{2,1,0:T(8,128)(2,1)S(1)} all-to-all(bf16[8,16,2048]{2,1,0:T(8,128)(2,1)S(1)} %broadcast_in_dim.14), channel_id=1, replica_groups={{0,2,4,6,17,19,21,23},{8,10,12,14,25,27,29,31},{16,18,20,22,1,3,5,7},{2..., dimensions={0} | all-to-all | bytes 1048576 | tf_op jit(solution)/shard_map/all_to_all | solution.py:169
  27.0 0.0 copy-start
  27.0 2.5 %collective-permute-start = (bf16[8,16,2048]{2,1,0:T(8,128)(2,1)S(1)}, bf16[8,16,2048]{2,1,0:T(8,128)(2,1)S(1)}, u32[]{:S(2)}, u32[]{:S(2)}) collective-permute-start(bf16[8,16,2048]{2,1,0:T(8,128)(2,1)S(1)} %all_to_all.10.own_ref), channel_id=1, source_target_pairs={{8,0},{9,1},{10,2},{11,3},{12,4},{13,5},{14,6},{15,7},{0,8},{1,9},... | collective-permute-start | bytes 1572872 | tf_op jit(solution)/shard_map/ppermute | solution.py:42
  29.5 3.9 %collective-permute-start.2 = (bf16[8,16,2048]{2,1,0:T(8,128)(2,1)S(1)}, bf16[8,16,2048]{2,1,0:T(8,128)(2,1)S(1)}, u32[]{:S(2)}, u32[]{:S(2)}) collective-permute-start(bf16[8,16,2048]{2,1,0:T(8,128)(2,1)S(1)} %all_to_all.10.own_ref), channel_id=1, source_target_pairs={{24,0},{25,1},{26,2},{27,3},{28,4},{29,5},{30,6},{31,7},{16,8},{17... | collective-permute-start | bytes 1572872 | tf_op jit(solution)/shard_map/ppermute | solution.py:42
  33.4 1.9 %collective-permute-start.3 = (bf16[5,16,2048]{2,1,0:T(8,128)(2,1)S(1)}, bf16[5,16,2048]{2,1,0:T(8,128)(2,1)S(1)}, u32[]{:S(2)}, u32[]{:S(2)}) collective-permute-start(bf16[5,16,2048]{2,1,0:T(8,128)(2,1)S(1)} %get-tuple-element.11), channel_id=1, source_target_pairs={{1,0},{0,1},{3,2},{2,3},{5,4},{4,5},{7,6},{6,7},{9,8},{8,9},{11,10... | collective-permute-start | bytes 983048 | tf_op jit(solution)/shard_map/ppermute | solution.py:42
  35.4 3.8 %collective-permute-start.4 = (bf16[3,16,2048]{2,1,0:T(8,128)(2,1)S(1)}, bf16[3,16,2048]{2,1,0:T(8,128)(2,1)S(1)}, u32[]{:S(2)}, u32[]{:S(2)}) collective-permute-start(bf16[3,16,2048]{2,1,0:T(8,128)(2,1)S(1)} %get-tuple-element.12), channel_id=1, source_target_pairs={{7,0},{2,1},{1,2},{4,3},{3,4},{6,5},{5,6},{0,7},{15,8},{10,9},{9,1... | collective-permute-start | bytes 589832 | tf_op jit(solution)/shard_map/ppermute | solution.py:42
  39.2 2.0 %collective-permute-done.right_ref = bf16[8,16,2048]{2,1,0:T(8,128)(2,1)S(1)} collective-permute-done((bf16[8,16,2048]{2,1,0:T(8,128)(2,1)S(1)}, bf16[8,16,2048]{2,1,0:T(8,128)(2,1)S(1)}, u32[]{:S(2)}, u32[]{:S(2)}) %collective-permute-start) | collective-permute-done | bytes 524320 | tf_op jit(solution)/shard_map/ppermute | solution.py:42
  41.2 0.0 copy-done
  41.2 1.4 %near.1 = (f32[2,64,896]{2,1,0:T(8,128)S(1)}, f32[2,64,896]{2,1,0:T(8,128)S(1)}) custom-call(bf16[8,16,2048]{2,1,0:T(8,128)(2,1)S(1)} %all_to_all.10.own_ref, bf16[8,16,2048]{2,1,0:T(8,128)(2,1)S(1)} %collective-permute-done.right_ref, bf16[1,2048,896]{2,1,0:T(8,128)(2,1)S(1)} %copy-done), custom_call_target="tpu_custom_call" | custom-call | flops 939524096 | bytes 5636096 | tf_op jit(solution)/shard_map/near/pallas_call | solution.py:150
  42.5 4.2 %collective-permute-start.1 = (f32[2,64,896]{2,1,0:T(8,128)S(1)}, f32[2,64,896]{2,1,0:T(8,128)S(1)}, u32[]{:S(2)}, u32[]{:S(2)}) collective-permute-start(f32[2,64,896]{2,1,0:T(8,128)S(1)} %get-tuple-element.10), channel_id=1, source_target_pairs={{0,32},{32,0},{64,96},{96,64},{128,160},{160,128},{192,224},{224,1... | collective-permute-start | bytes 1376264 | tf_op jit(solution)/shard_map/ppermute | solution.py:181
  46.8 0.0 collective-permute-done.4.down_ref
  46.8 0.0 collective-permute-done.3.up_ref
  46.8 0.0 collective-permute-done.2.left_ref
  46.8 0.7 far_theirs.1
  47.5 2.7 %collective-permute-start.5 = (f32[2,64,896]{2,1,0:T(8,128)S(1)}, f32[2,64,896]{2,1,0:T(8,128)S(1)}, u32[]{:S(2)}, u32[]{:S(2)}) collective-permute-start(f32[2,64,896]{2,1,0:T(8,128)S(1)} %far_theirs.1), channel_id=1, source_target_pairs={{0,32},{32,0},{64,96},{96,64},{128,160},{160,128},{192,224},{224,1... | collective-permute-start | bytes 1376264 | tf_op jit(solution)/shard_map/ppermute | solution.py:183
  50.3 0.7 far_ours.1.far_ours_ref
  51.0 0.0 collective-permute-done.1.near_given_ref
  51.0 0.7 collective-permute-done.5.far_given_ref
  51.7 0.3 pack.1
  52.0 25.0 %all_to_all.11.in_ref = s16[8,240,128]{2,1,0:T(8,128)(2,1)S(1)} all-to-all(s16[8,240,128]{2,1,0:T(8,128)(2,1)S(1)} %pack.1), channel_id=1, replica_groups={{0,448,64,384,128,320,192,256},{257,193,321,129,385,65,449,1},{2,450,66..., dimensions={0} | all-to-all | bytes 983040 | tf_op jit(solution)/shard_map/all_to_all | solution.py:187
  77.0 0.8 unpack_sum.1
  (3 shorter events, 0.1 us)
Async XLA Ops:
  27.0 14.2 %copy-start = (bf16[1,2048,896]{2,1,0:T(8,128)(2,1)S(1)}, bf16[1,2048,896]{2,1,0:T(8,128)(2,1)}, u32[]{:S(2)}) copy-start(bf16[1,2048,896]{2,1,0:T(8,128)(2,1)} %integrals_ref.5) | copy-start | bytes 11010052
  27.0 14.2 %collective-permute-start = (bf16[8,16,2048]{2,1,0:T(8,128)(2,1)S(1)}, bf16[8,16,2048]{2,1,0:T(8,128)(2,1)S(1)}, u32[]{:S(2)}, u32[]{:S(2)}) collective-permute-start(bf16[8,16,2048]{2,1,0:T(8,128)(2,1)S(1)} %all_to_all.10.own_ref), channel_id=1, source_target_pairs={{8,0},{9,1},{10,2},{11,3},{12,4},{13,5},{14,6},{15,7},{0,8},{1,9},... | collective-permute-start | bytes 1572872 | tf_op jit(solution)/shard_map/ppermute | solution.py:42
  29.5 17.3 %collective-permute-start.2 = (bf16[8,16,2048]{2,1,0:T(8,128)(2,1)S(1)}, bf16[8,16,2048]{2,1,0:T(8,128)(2,1)S(1)}, u32[]{:S(2)}, u32[]{:S(2)}) collective-permute-start(bf16[8,16,2048]{2,1,0:T(8,128)(2,1)S(1)} %all_to_all.10.own_ref), channel_id=1, source_target_pairs={{24,0},{25,1},{26,2},{27,3},{28,4},{29,5},{30,6},{31,7},{16,8},{17... | collective-permute-start | bytes 1572872 | tf_op jit(solution)/shard_map/ppermute | solution.py:42
  33.4 13.4 %collective-permute-start.3 = (bf16[5,16,2048]{2,1,0:T(8,128)(2,1)S(1)}, bf16[5,16,2048]{2,1,0:T(8,128)(2,1)S(1)}, u32[]{:S(2)}, u32[]{:S(2)}) collective-permute-start(bf16[5,16,2048]{2,1,0:T(8,128)(2,1)S(1)} %get-tuple-element.11), channel_id=1, source_target_pairs={{1,0},{0,1},{3,2},{2,3},{5,4},{4,5},{7,6},{6,7},{9,8},{8,9},{11,10... | collective-permute-start | bytes 983048 | tf_op jit(solution)/shard_map/ppermute | solution.py:42
  35.4 11.4 %collective-permute-start.4 = (bf16[3,16,2048]{2,1,0:T(8,128)(2,1)S(1)}, bf16[3,16,2048]{2,1,0:T(8,128)(2,1)S(1)}, u32[]{:S(2)}, u32[]{:S(2)}) collective-permute-start(bf16[3,16,2048]{2,1,0:T(8,128)(2,1)S(1)} %get-tuple-element.12), channel_id=1, source_target_pairs={{7,0},{2,1},{1,2},{4,3},{3,4},{6,5},{5,6},{0,7},{15,8},{10,9},{9,1... | collective-permute-start | bytes 589832 | tf_op jit(solution)/shard_map/ppermute | solution.py:42
  42.5 8.5 %collective-permute-start.1 = (f32[2,64,896]{2,1,0:T(8,128)S(1)}, f32[2,64,896]{2,1,0:T(8,128)S(1)}, u32[]{:S(2)}, u32[]{:S(2)}) collective-permute-start(f32[2,64,896]{2,1,0:T(8,128)S(1)} %get-tuple-element.10), channel_id=1, source_target_pairs={{0,32},{32,0},{64,96},{96,64},{128,160},{160,128},{192,224},{224,1... | collective-permute-start | bytes 1376264 | tf_op jit(solution)/shard_map/ppermute | solution.py:181
  47.5 4.2 %collective-permute-start.5 = (f32[2,64,896]{2,1,0:T(8,128)S(1)}, f32[2,64,896]{2,1,0:T(8,128)S(1)}, u32[]{:S(2)}, u32[]{:S(2)}) collective-permute-start(f32[2,64,896]{2,1,0:T(8,128)S(1)} %far_theirs.1), channel_id=1, source_target_pairs={{0,32},{32,0},{64,96},{96,64},{128,160},{160,128},{192,224},{224,1... | collective-permute-start | bytes 1376264 | tf_op jit(solution)/shard_map/ppermute | solution.py:183

commit v7 on v6

--- a/solution.py
+++ b/solution.py
@@ -33,13 +33,14 @@
 Z_GROUPS = z_groups()
 
 
-def exchange(block, dx, dy):
+def exchange(block, dx, dy, flip=0):
     pairs = []
-    for t in range(X * Y):
-        x, y = t // Y, t % Y
-        sign = 1 - 2 * ((x if dx else y) % 2)
-        pairs.append((tr_of(x + sign * dx, y + sign * dy), t))
-    return lax.ppermute(block, "tr", pairs)
+    for g in range(2 * Z):
+        for t in range(X * Y):
+            x, y = t // Y, t % Y
+            sign = 1 - 2 * (((x if dx else y) + flip * g) % 2)
+            pairs.append((g * X * Y + tr_of(x + sign * dx, y + sign * dy), g * X * Y + t))
+    return lax.ppermute(block, ("grp", "tr"), pairs)
 
 
 def multiply(blocks, integrals_ref):
@@ -51,9 +52,8 @@
     return lax.rem(lax.axis_index("grp"), 2)
 
 
-def split(own_ref, low_ref, high_ref):
-    low_ref[...] = own_ref[:MOST]
-    high_ref[...] = own_ref[MOST:]
+def split(own_ref, copy_ref):
+    copy_ref[...] = own_ref[...]
 
 
 def near_product(own_ref, right_ref, integrals_ref, ours_ref, theirs_ref):
@@ -75,11 +75,10 @@
                 theirs_ref[d, span] = values
 
 
-def far_product(side, left_ref, up_ref, down_ref, integrals_ref, out_ref):
+def far_product(side, left_ref, up_ref, integrals_ref, out_ref):
     core = lax.rem(this_core() + side, 2)
     blocks = [left_ref[core + 2 * i] for i in range(4)]
-    across = [up_ref[i] for i in range(MOST)] + [down_ref[i] for i in range(8 - MOST)]
-    blocks += [jnp.where(core == 0, across[2 * i], across[2 * i + 1]) for i in range(4)]
+    blocks += [up_ref[core + 2 * i] for i in range(4)]
     product = multiply(blocks, integrals_ref)
     count = out_ref.shape[1]
     out_ref[0] = product[:count]
@@ -106,7 +105,7 @@
                         span = pl.ds((2 * b + h) * rows, rows)
                         value = ours[at][span, :] + given[at][span, :]
                         top = jnp.max(jnp.abs(value), axis=1, keepdims=True)
-                        exponent = jnp.ceil(jnp.log2(jnp.maximum(top, 2.0**-100)))
+                        exponent = jnp.ceil(jnp.log2(jnp.maximum(top, 2.0**-110)))
                         scaled = jnp.clip(jnp.round(value * jnp.exp2(15.0 - exponent)), -32767.0, 32767.0)
                         number = scaled.astype(jnp.int32).astype(jnp.int16)
                         for g in range(groups):
@@ -169,19 +168,18 @@
     own = lax.all_to_all(copies, "tr", 0, 0, axis_index_groups=CLASS_GROUPS)
     right = exchange(own, 1, 0)
     left = exchange(own, -1, 0)
-    parts = tuple(jax.ShapeDtypeStruct((n, rows, depth), own.dtype) for n in (MOST, 8 - MOST))
-    low, high = call(split, parts, "split", 4, 4000000000)(own)
-    up = exchange(low, 0, 1)
-    down = exchange(high, 0, -1)
+    parts = jax.ShapeDtypeStruct(own.shape, own.dtype)
+    copy = call(split, parts, "split", 4, 4000000000)(own)
+    up = exchange(copy, 0, 1, 1)
 
     side = jax.ShapeDtypeStruct((2, 4 * rows, width), jnp.float32)
     work = 2 * 8 * rows * depth * width
     swap = [(g, g ^ 1) for g in range(2 * Z)]
     near, near_theirs = call(near_product, (side, side), "near", LIMIT_DOT, 2 * work)(own, right, integrals)
     near_given = lax.ppermute(near_theirs, "grp", swap)
-    far_theirs = call(functools.partial(far_product, 1), side, "far_theirs", LIMIT_DOT, work)(left, up, down, integrals)
+    far_theirs = call(functools.partial(far_product, 1), side, "far_theirs", LIMIT_DOT, work)(left, up, integrals)
     far_given = lax.ppermute(far_theirs, "grp", swap)
-    far = call(functools.partial(far_product, 0), side, "far_ours", LIMIT_DOT, work)(left, up, down, integrals)
+    far = call(functools.partial(far_product, 0), side, "far_ours", LIMIT_DOT, work)(left, up, integrals)
     block = jax.ShapeDtypeStruct((Z, 2 * rows * (width // LANES) + rows, LANES), jnp.int16)
     packed = call(pack, block, "pack", 4)(near, near_given, far, far_given)
     arrived = lax.all_to_all(packed, ("grp", "tr"), 0, 0, axis_index_groups=Z_GROUPS)

time: 78.3 us -> 77.9 us (level)
  starting transfers between devices: 19.1 us -> 15.3 us
  waiting for transfers between devices: 2.68 us -> 6.02 us
    ppermute x4 -> x3, waiting for transfers between devices: 1.99 us -> 5.13 us  [exchange(): return lax.ppermute(block, ('grp', 'tr'), pairs)]
    ppermute x4 -> x3, starting transfers between devices: 12.1 us -> 8.96 us  [exchange(): return lax.ppermute(block, ('grp', 'tr'), pairs)]
  transfers between devices with their start and end apart: 6 -> 5, of which waited for: 2 -> 2; matrix products, arithmetic and copies ran while one was open for 0% -> 0% of each run, Pallas kernels for 4% -> 4%
where the time goes in v7:
time: 77.9 us; the launch traced here: 77.3 us
  blocking collectives  50.4 us (65%)
  starting transfers between devices  15.3 us (20%)
  waiting for transfers between devices  6.02 us (8%)
  Pallas kernels  3.88 us (5%)
  other arithmetic  0.86 us (1%)
    all_to_all x1, blocking collectives, on_device(): own = lax.all_to_all(copies, 'tr', 0, 0, axis_index_groups=CLASS_GROUPS)  25.4 us
    all_to_all x1, blocking collectives, on_device(): lax.all_to_all(packed, ('grp', 'tr'), 0, 0, axis_index_groups=Z_GROUPS)  25 us
    ppermute x3, starting transfers between devices, exchange(): return lax.ppermute(block, ('grp', 'tr'), pairs)  8.96 us
    ppermute x3, waiting for transfers between devices, exchange(): return lax.ppermute(block, ('grp', 'tr'), pairs)  5.13 us
    ppermute x1, starting transfers between devices, on_device(): near_given = lax.ppermute(near_theirs, 'grp', swap)  4.24 us
    pallas_call x6, Pallas kernels, run(): pl.pallas_call(kernel, out_shape=shapes, in_specs=[vmem] * len(operands),...  3.88 us
    ppermute x1, starting transfers between devices, on_device(): far_given = lax.ppermute(far_theirs, 'grp', swap)  2.09 us
  transfers between devices with their start and end apart: 5, of which 2 were waited for; matrix products, arithmetic and copies ran while one was open for 0% of the time, Pallas kernels for 4%

profile of v7, /device:TPU:1, one launch (start us, length us, event | category | flops | bytes accessed | tf_op | source)
XLA Modules:
  0.0 77.3 jit_solution(13789799896429538910)
XLA Ops:
  0.7 0.9 %bitcast_select_fusion = bf16[16,2048]{1,0:T(8,128)(2,1)S(1)} fusion(bf16[16,1,2048]{2,0,1:T(8,128)(2,1)} %param.3, pred[2048]{0:T(1024)(128)(4,1)S(1)} %iota_compare_fusion), kind=kLoop, calls=%fused_computation | loop fusion | flops 32768 | bytes 133120 | tf_op jit(solution)/shard_map/jit(_where)/select_n | solution.py:166
  1.6 25.4 %all_to_all.10.own_ref = bf16[8,16,2048]{2,1,0:T(8,128)(2,1)S(1)} all-to-all(bf16[8,16,2048]{2,1,0:T(8,128)(2,1)S(1)} %broadcast_in_dim.14), channel_id=1, replica_groups={{0,2,4,6,17,19,21,23},{8,10,12,14,25,27,29,31},{16,18,20,22,1,3,5,7},{2..., dimensions={0} | all-to-all | bytes 1048576 | tf_op jit(solution)/shard_map/all_to_all | solution.py:168
  27.0 0.0 copy-start
  27.0 2.5 %collective-permute-start = (bf16[8,16,2048]{2,1,0:T(8,128)(2,1)S(1)}, bf16[8,16,2048]{2,1,0:T(8,128)(2,1)S(1)}, u32[]{:S(2)}, u32[]{:S(2)}) collective-permute-start(bf16[8,16,2048]{2,1,0:T(8,128)(2,1)S(1)} %all_to_all.10.own_ref), channel_id=1, source_target_pairs={{8,0},{9,1},{10,2},{11,3},{12,4},{13,5},{14,6},{15,7},{0,8},{1,9},... | collective-permute-start | bytes 1572872 | tf_op jit(solution)/shard_map/ppermute | solution.py:43
  29.5 3.9 %collective-permute-start.2 = (bf16[8,16,2048]{2,1,0:T(8,128)(2,1)S(1)}, bf16[8,16,2048]{2,1,0:T(8,128)(2,1)S(1)}, u32[]{:S(2)}, u32[]{:S(2)}) collective-permute-start(bf16[8,16,2048]{2,1,0:T(8,128)(2,1)S(1)} %all_to_all.10.own_ref), channel_id=1, source_target_pairs={{24,0},{25,1},{26,2},{27,3},{28,4},{29,5},{30,6},{31,7},{16,8},{17... | collective-permute-start | bytes 1572872 | tf_op jit(solution)/shard_map/ppermute | solution.py:43
  33.4 2.6 %collective-permute-start.3 = (bf16[8,16,2048]{2,1,0:T(8,128)(2,1)S(1)}, bf16[8,16,2048]{2,1,0:T(8,128)(2,1)S(1)}, u32[]{:S(2)}, u32[]{:S(2)}) collective-permute-start(bf16[8,16,2048]{2,1,0:T(8,128)(2,1)S(1)} %split.1), channel_id=1, source_target_pairs={{1,0},{0,1},{3,2},{2,3},{5,4},{4,5},{7,6},{6,7},{9,8},{8,9},{11,10... | collective-permute-start | bytes 1572872 | tf_op jit(solution)/shard_map/ppermute | solution.py:43
  36.0 5.1 %collective-permute-done.right_ref = bf16[8,16,2048]{2,1,0:T(8,128)(2,1)S(1)} collective-permute-done((bf16[8,16,2048]{2,1,0:T(8,128)(2,1)S(1)}, bf16[8,16,2048]{2,1,0:T(8,128)(2,1)S(1)}, u32[]{:S(2)}, u32[]{:S(2)}) %collective-permute-start) | collective-permute-done | bytes 524320 | tf_op jit(solution)/shard_map/ppermute | solution.py:43
  41.2 0.0 copy-done
  41.2 1.4 %near.1 = (f32[2,64,896]{2,1,0:T(8,128)S(1)}, f32[2,64,896]{2,1,0:T(8,128)S(1)}) custom-call(bf16[8,16,2048]{2,1,0:T(8,128)(2,1)S(1)} %all_to_all.10.own_ref, bf16[8,16,2048]{2,1,0:T(8,128)(2,1)S(1)} %collective-permute-done.right_ref, bf16[1,2048,896]{2,1,0:T(8,128)(2,1)S(1)} %copy-done), custom_call_target="tpu_custom_call" | custom-call | flops 939524096 | bytes 5636096 | tf_op jit(solution)/shard_map/near/pallas_call | solution.py:149
  42.5 4.2 %collective-permute-start.1 = (f32[2,64,896]{2,1,0:T(8,128)S(1)}, f32[2,64,896]{2,1,0:T(8,128)S(1)}, u32[]{:S(2)}, u32[]{:S(2)}) collective-permute-start(f32[2,64,896]{2,1,0:T(8,128)S(1)} %get-tuple-element.8), channel_id=1, source_target_pairs={{0,32},{32,0},{64,96},{96,64},{128,160},{160,128},{192,224},{224,1... | collective-permute-start | bytes 1376264 | tf_op jit(solution)/shard_map/ppermute | solution.py:179
  46.8 0.0 collective-permute-done.2.left_ref
  46.8 0.0 collective-permute-done.3.up_ref
  46.8 0.7 far_theirs.1
  47.5 2.1 %collective-permute-start.4 = (f32[2,64,896]{2,1,0:T(8,128)S(1)}, f32[2,64,896]{2,1,0:T(8,128)S(1)}, u32[]{:S(2)}, u32[]{:S(2)}) collective-permute-start(f32[2,64,896]{2,1,0:T(8,128)S(1)} %far_theirs.1), channel_id=1, source_target_pairs={{0,32},{32,0},{64,96},{96,64},{128,160},{160,128},{192,224},{224,1... | collective-permute-start | bytes 1376264 | tf_op jit(solution)/shard_map/ppermute | solution.py:181
  49.6 0.7 far_ours.1.far_ours_ref
  50.4 0.0 collective-permute-done.1.near_given_ref
  50.4 0.9 %collective-permute-done.4.far_given_ref = f32[2,64,896]{2,1,0:T(8,128)S(1)} collective-permute-done((f32[2,64,896]{2,1,0:T(8,128)S(1)}, f32[2,64,896]{2,1,0:T(8,128)S(1)}, u32[]{:S(2)}, u32[]{:S(2)}) %collective-permute-start.4) | collective-permute-done | bytes 458784 | tf_op jit(solution)/shard_map/ppermute | solution.py:181
  51.2 0.3 pack.1
  51.5 25.0 %all_to_all.11.in_ref = s16[8,240,128]{2,1,0:T(8,128)(2,1)S(1)} all-to-all(s16[8,240,128]{2,1,0:T(8,128)(2,1)S(1)} %pack.1), channel_id=1, replica_groups={{0,448,64,384,128,320,192,256},{257,193,321,129,385,65,449,1},{2,450,66..., dimensions={0} | all-to-all | bytes 983040 | tf_op jit(solution)/shard_map/all_to_all | solution.py:185
  76.5 0.8 unpack_sum.1
  (3 shorter events, 0.1 us)
Async XLA Ops:
  27.0 14.2 %copy-start = (bf16[1,2048,896]{2,1,0:T(8,128)(2,1)S(1)}, bf16[1,2048,896]{2,1,0:T(8,128)(2,1)}, u32[]{:S(2)}) copy-start(bf16[1,2048,896]{2,1,0:T(8,128)(2,1)} %integrals_ref.5) | copy-start | bytes 11010052
  27.0 14.2 %collective-permute-start = (bf16[8,16,2048]{2,1,0:T(8,128)(2,1)S(1)}, bf16[8,16,2048]{2,1,0:T(8,128)(2,1)S(1)}, u32[]{:S(2)}, u32[]{:S(2)}) collective-permute-start(bf16[8,16,2048]{2,1,0:T(8,128)(2,1)S(1)} %all_to_all.10.own_ref), channel_id=1, source_target_pairs={{8,0},{9,1},{10,2},{11,3},{12,4},{13,5},{14,6},{15,7},{0,8},{1,9},... | collective-permute-start | bytes 1572872 | tf_op jit(solution)/shard_map/ppermute | solution.py:43
  29.5 17.3 %collective-permute-start.2 = (bf16[8,16,2048]{2,1,0:T(8,128)(2,1)S(1)}, bf16[8,16,2048]{2,1,0:T(8,128)(2,1)S(1)}, u32[]{:S(2)}, u32[]{:S(2)}) collective-permute-start(bf16[8,16,2048]{2,1,0:T(8,128)(2,1)S(1)} %all_to_all.10.own_ref), channel_id=1, source_target_pairs={{24,0},{25,1},{26,2},{27,3},{28,4},{29,5},{30,6},{31,7},{16,8},{17... | collective-permute-start | bytes 1572872 | tf_op jit(solution)/shard_map/ppermute | solution.py:43
  33.4 13.4 %collective-permute-start.3 = (bf16[8,16,2048]{2,1,0:T(8,128)(2,1)S(1)}, bf16[8,16,2048]{2,1,0:T(8,128)(2,1)S(1)}, u32[]{:S(2)}, u32[]{:S(2)}) collective-permute-start(bf16[8,16,2048]{2,1,0:T(8,128)(2,1)S(1)} %split.1), channel_id=1, source_target_pairs={{1,0},{0,1},{3,2},{2,3},{5,4},{4,5},{7,6},{6,7},{9,8},{8,9},{11,10... | collective-permute-start | bytes 1572872 | tf_op jit(solution)/shard_map/ppermute | solution.py:43
  42.5 7.8 %collective-permute-start.1 = (f32[2,64,896]{2,1,0:T(8,128)S(1)}, f32[2,64,896]{2,1,0:T(8,128)S(1)}, u32[]{:S(2)}, u32[]{:S(2)}) collective-permute-start(f32[2,64,896]{2,1,0:T(8,128)S(1)} %get-tuple-element.8), channel_id=1, source_target_pairs={{0,32},{32,0},{64,96},{96,64},{128,160},{160,128},{192,224},{224,1... | collective-permute-start | bytes 1376264 | tf_op jit(solution)/shard_map/ppermute | solution.py:179
  47.5 3.7 %collective-permute-start.4 = (f32[2,64,896]{2,1,0:T(8,128)S(1)}, f32[2,64,896]{2,1,0:T(8,128)S(1)}, u32[]{:S(2)}, u32[]{:S(2)}) collective-permute-start(f32[2,64,896]{2,1,0:T(8,128)S(1)} %far_theirs.1), channel_id=1, source_target_pairs={{0,32},{32,0},{64,96},{96,64},{128,160},{160,128},{192,224},{224,1... | collective-permute-start | bytes 1376264 | tf_op jit(solution)/shard_map/ppermute | solution.py:181

commit v8 on v7

--- a/solution.py
+++ b/solution.py
@@ -52,7 +52,7 @@
     return lax.rem(lax.axis_index("grp"), 2)
 
 
-def split(own_ref, copy_ref):
+def copy_own(own_ref, copy_ref):
     copy_ref[...] = own_ref[...]
 
 
@@ -105,8 +105,8 @@
                         span = pl.ds((2 * b + h) * rows, rows)
                         value = ours[at][span, :] + given[at][span, :]
                         top = jnp.max(jnp.abs(value), axis=1, keepdims=True)
-                        exponent = jnp.ceil(jnp.log2(jnp.maximum(top, 2.0**-110)))
-                        scaled = jnp.clip(jnp.round(value * jnp.exp2(15.0 - exponent)), -32767.0, 32767.0)
+                        exponent = jnp.ceil(FINE * jnp.log2(jnp.maximum(top, 2.0**-110)))
+                        scaled = jnp.clip(jnp.round(value * jnp.exp2(15.0 - exponent / FINE)), -32767.0, 32767.0)
                         number = scaled.astype(jnp.int32).astype(jnp.int16)
                         for g in range(groups):
                             lane = pl.ds((2 * g + b) * rows, rows)
@@ -124,7 +124,7 @@
     steps = []
     for p in range(planes):
         exponent = in_ref[p, pl.ds(2 * groups * rows, rows), :].astype(jnp.int32).astype(jnp.float32)
-        step = jnp.exp2(exponent - 15.0)
+        step = jnp.exp2(exponent / FINE - 15.0)
         steps.append((step[:, :1], step[:, lanes // 2 : lanes // 2 + 1]))
     for b in range(2):
         for g in range(groups):
@@ -136,8 +136,8 @@
 
 
 LANES = 128
+FINE = 64
 LIMIT_DOT = 8
-MOST = 5
 
 
 def call(kernel, shapes, name, limit, flops=0):
@@ -169,7 +169,7 @@
     right = exchange(own, 1, 0)
     left = exchange(own, -1, 0)
     parts = jax.ShapeDtypeStruct(own.shape, own.dtype)
-    copy = call(split, parts, "split", 4, 4000000000)(own)
+    copy = call(copy_own, parts, "copy_own", 4, 4000000000)(own)
     up = exchange(copy, 0, 1, 1)
 
     side = jax.ShapeDtypeStruct((2, 4 * rows, width), jnp.float32)

time: 77.9 us -> 77.9 us (level)
  no operation moved by 1% of the time
where the time goes in v8:
time: 77.9 us; the launch traced here: 77.3 us
  blocking collectives  50.4 us (65%)
  starting transfers between devices  15.3 us (20%)
  waiting for transfers between devices  6.02 us (8%)
  Pallas kernels  3.9 us (5%)
  other arithmetic  0.86 us (1%)
    all_to_all x1, blocking collectives, on_device(): own = lax.all_to_all(copies, 'tr', 0, 0, axis_index_groups=CLASS_GROUPS)  25.4 us
    all_to_all x1, blocking collectives, on_device(): lax.all_to_all(packed, ('grp', 'tr'), 0, 0, axis_index_groups=Z_GROUPS)  25 us
    ppermute x3, starting transfers between devices, exchange(): return lax.ppermute(block, ('grp', 'tr'), pairs)  8.96 us
    ppermute x3, waiting for transfers between devices, exchange(): return lax.ppermute(block, ('grp', 'tr'), pairs)  5.13 us
    ppermute x1, starting transfers between devices, on_device(): near_given = lax.ppermute(near_theirs, 'grp', swap)  4.24 us
    pallas_call x6, Pallas kernels, run(): pl.pallas_call(kernel, out_shape=shapes, in_specs=[vmem] * len(operands),...  3.9 us
    ppermute x1, starting transfers between devices, on_device(): far_given = lax.ppermute(far_theirs, 'grp', swap)  2.09 us
  transfers between devices with their start and end apart: 5, of which 2 were waited for; matrix products, arithmetic and copies ran while one was open for 0% of the time, Pallas kernels for 4%

profile of v8, /device:TPU:1, one launch (start us, length us, event | category | flops | bytes accessed | tf_op | source)
XLA Modules:
  0.0 77.3 jit_solution(2177827480205980050)
XLA Ops:
  0.7 0.9 %bitcast_select_fusion = bf16[16,2048]{1,0:T(8,128)(2,1)S(1)} fusion(bf16[16,1,2048]{2,0,1:T(8,128)(2,1)} %param.3, pred[2048]{0:T(1024)(128)(4,1)S(1)} %iota_compare_fusion), kind=kLoop, calls=%fused_computation | loop fusion | flops 32768 | bytes 133120 | tf_op jit(solution)/shard_map/jit(_where)/select_n | solution.py:166
  1.6 25.4 %all_to_all.10.own_ref = bf16[8,16,2048]{2,1,0:T(8,128)(2,1)S(1)} all-to-all(bf16[8,16,2048]{2,1,0:T(8,128)(2,1)S(1)} %broadcast_in_dim.14), channel_id=1, replica_groups={{0,2,4,6,17,19,21,23},{8,10,12,14,25,27,29,31},{16,18,20,22,1,3,5,7},{2..., dimensions={0} | all-to-all | bytes 1048576 | tf_op jit(solution)/shard_map/all_to_all | solution.py:168
  27.0 0.0 copy-start
  27.0 2.5 %collective-permute-start = (bf16[8,16,2048]{2,1,0:T(8,128)(2,1)S(1)}, bf16[8,16,2048]{2,1,0:T(8,128)(2,1)S(1)}, u32[]{:S(2)}, u32[]{:S(2)}) collective-permute-start(bf16[8,16,2048]{2,1,0:T(8,128)(2,1)S(1)} %all_to_all.10.own_ref), channel_id=1, source_target_pairs={{8,0},{9,1},{10,2},{11,3},{12,4},{13,5},{14,6},{15,7},{0,8},{1,9},... | collective-permute-start | bytes 1572872 | tf_op jit(solution)/shard_map/ppermute | solution.py:43
  29.5 3.9 %collective-permute-start.2 = (bf16[8,16,2048]{2,1,0:T(8,128)(2,1)S(1)}, bf16[8,16,2048]{2,1,0:T(8,128)(2,1)S(1)}, u32[]{:S(2)}, u32[]{:S(2)}) collective-permute-start(bf16[8,16,2048]{2,1,0:T(8,128)(2,1)S(1)} %all_to_all.10.own_ref), channel_id=1, source_target_pairs={{24,0},{25,1},{26,2},{27,3},{28,4},{29,5},{30,6},{31,7},{16,8},{17... | collective-permute-start | bytes 1572872 | tf_op jit(solution)/shard_map/ppermute | solution.py:43
  33.4 2.6 %collective-permute-start.3 = (bf16[8,16,2048]{2,1,0:T(8,128)(2,1)S(1)}, bf16[8,16,2048]{2,1,0:T(8,128)(2,1)S(1)}, u32[]{:S(2)}, u32[]{:S(2)}) collective-permute-start(bf16[8,16,2048]{2,1,0:T(8,128)(2,1)S(1)} %copy_own.1), channel_id=1, source_target_pairs={{1,0},{0,1},{3,2},{2,3},{5,4},{4,5},{7,6},{6,7},{9,8},{8,9},{11,10... | collective-permute-start | bytes 1572872 | tf_op jit(solution)/shard_map/ppermute | solution.py:43
  36.0 5.1 %collective-permute-done.right_ref = bf16[8,16,2048]{2,1,0:T(8,128)(2,1)S(1)} collective-permute-done((bf16[8,16,2048]{2,1,0:T(8,128)(2,1)S(1)}, bf16[8,16,2048]{2,1,0:T(8,128)(2,1)S(1)}, u32[]{:S(2)}, u32[]{:S(2)}) %collective-permute-start) | collective-permute-done | bytes 524320 | tf_op jit(solution)/shard_map/ppermute | solution.py:43
  41.2 0.0 copy-done
  41.2 1.4 %near.1 = (f32[2,64,896]{2,1,0:T(8,128)S(1)}, f32[2,64,896]{2,1,0:T(8,128)S(1)}) custom-call(bf16[8,16,2048]{2,1,0:T(8,128)(2,1)S(1)} %all_to_all.10.own_ref, bf16[8,16,2048]{2,1,0:T(8,128)(2,1)S(1)} %collective-permute-done.right_ref, bf16[1,2048,896]{2,1,0:T(8,128)(2,1)S(1)} %copy-done), custom_call_target="tpu_custom_call" | custom-call | flops 939524096 | bytes 5636096 | tf_op jit(solution)/shard_map/near/pallas_call | solution.py:149
  42.5 4.2 %collective-permute-start.1 = (f32[2,64,896]{2,1,0:T(8,128)S(1)}, f32[2,64,896]{2,1,0:T(8,128)S(1)}, u32[]{:S(2)}, u32[]{:S(2)}) collective-permute-start(f32[2,64,896]{2,1,0:T(8,128)S(1)} %get-tuple-element.8), channel_id=1, source_target_pairs={{0,32},{32,0},{64,96},{96,64},{128,160},{160,128},{192,224},{224,1... | collective-permute-start | bytes 1376264 | tf_op jit(solution)/shard_map/ppermute | solution.py:179
  46.8 0.0 collective-permute-done.2.left_ref
  46.8 0.0 collective-permute-done.3.up_ref
  46.8 0.7 far_theirs.1
  47.5 2.1 %collective-permute-start.4 = (f32[2,64,896]{2,1,0:T(8,128)S(1)}, f32[2,64,896]{2,1,0:T(8,128)S(1)}, u32[]{:S(2)}, u32[]{:S(2)}) collective-permute-start(f32[2,64,896]{2,1,0:T(8,128)S(1)} %far_theirs.1), channel_id=1, source_target_pairs={{0,32},{32,0},{64,96},{96,64},{128,160},{160,128},{192,224},{224,1... | collective-permute-start | bytes 1376264 | tf_op jit(solution)/shard_map/ppermute | solution.py:181
  49.6 0.7 far_ours.1.far_ours_ref
  50.4 0.0 collective-permute-done.1.near_given_ref
  50.4 0.9 %collective-permute-done.4.far_given_ref = f32[2,64,896]{2,1,0:T(8,128)S(1)} collective-permute-done((f32[2,64,896]{2,1,0:T(8,128)S(1)}, f32[2,64,896]{2,1,0:T(8,128)S(1)}, u32[]{:S(2)}, u32[]{:S(2)}) %collective-permute-start.4) | collective-permute-done | bytes 458784 | tf_op jit(solution)/shard_map/ppermute | solution.py:181
  51.2 0.3 pack.1
  51.5 25.0 %all_to_all.11.in_ref = s16[8,240,128]{2,1,0:T(8,128)(2,1)S(1)} all-to-all(s16[8,240,128]{2,1,0:T(8,128)(2,1)S(1)} %pack.1), channel_id=1, replica_groups={{0,448,64,384,128,320,192,256},{257,193,321,129,385,65,449,1},{2,450,66..., dimensions={0} | all-to-all | bytes 983040 | tf_op jit(solution)/shard_map/all_to_all | solution.py:185
  76.5 0.8 unpack_sum.1
  (3 shorter events, 0.1 us)
Async XLA Ops:
  27.0 14.2 %copy-start = (bf16[1,2048,896]{2,1,0:T(8,128)(2,1)S(1)}, bf16[1,2048,896]{2,1,0:T(8,128)(2,1)}, u32[]{:S(2)}) copy-start(bf16[1,2048,896]{2,1,0:T(8,128)(2,1)} %integrals_ref.5) | copy-start | bytes 11010052
  27.0 14.2 %collective-permute-start = (bf16[8,16,2048]{2,1,0:T(8,128)(2,1)S(1)}, bf16[8,16,2048]{2,1,0:T(8,128)(2,1)S(1)}, u32[]{:S(2)}, u32[]{:S(2)}) collective-permute-start(bf16[8,16,2048]{2,1,0:T(8,128)(2,1)S(1)} %all_to_all.10.own_ref), channel_id=1, source_target_pairs={{8,0},{9,1},{10,2},{11,3},{12,4},{13,5},{14,6},{15,7},{0,8},{1,9},... | collective-permute-start | bytes 1572872 | tf_op jit(solution)/shard_map/ppermute | solution.py:43
  29.5 17.3 %collective-permute-start.2 = (bf16[8,16,2048]{2,1,0:T(8,128)(2,1)S(1)}, bf16[8,16,2048]{2,1,0:T(8,128)(2,1)S(1)}, u32[]{:S(2)}, u32[]{:S(2)}) collective-permute-start(bf16[8,16,2048]{2,1,0:T(8,128)(2,1)S(1)} %all_to_all.10.own_ref), channel_id=1, source_target_pairs={{24,0},{25,1},{26,2},{27,3},{28,4},{29,5},{30,6},{31,7},{16,8},{17... | collective-permute-start | bytes 1572872 | tf_op jit(solution)/shard_map/ppermute | solution.py:43
  33.4 13.4 %collective-permute-start.3 = (bf16[8,16,2048]{2,1,0:T(8,128)(2,1)S(1)}, bf16[8,16,2048]{2,1,0:T(8,128)(2,1)S(1)}, u32[]{:S(2)}, u32[]{:S(2)}) collective-permute-start(bf16[8,16,2048]{2,1,0:T(8,128)(2,1)S(1)} %copy_own.1), channel_id=1, source_target_pairs={{1,0},{0,1},{3,2},{2,3},{5,4},{4,5},{7,6},{6,7},{9,8},{8,9},{11,10... | collective-permute-start | bytes 1572872 | tf_op jit(solution)/shard_map/ppermute | solution.py:43
  42.5 7.8 %collective-permute-start.1 = (f32[2,64,896]{2,1,0:T(8,128)S(1)}, f32[2,64,896]{2,1,0:T(8,128)S(1)}, u32[]{:S(2)}, u32[]{:S(2)}) collective-permute-start(f32[2,64,896]{2,1,0:T(8,128)S(1)} %get-tuple-element.8), channel_id=1, source_target_pairs={{0,32},{32,0},{64,96},{96,64},{128,160},{160,128},{192,224},{224,1... | collective-permute-start | bytes 1376264 | tf_op jit(solution)/shard_map/ppermute | solution.py:179
  47.5 3.7 %collective-permute-start.4 = (f32[2,64,896]{2,1,0:T(8,128)S(1)}, f32[2,64,896]{2,1,0:T(8,128)S(1)}, u32[]{:S(2)}, u32[]{:S(2)}) collective-permute-start(f32[2,64,896]{2,1,0:T(8,128)S(1)} %far_theirs.1), channel_id=1, source_target_pairs={{0,32},{32,0},{64,96},{96,64},{128,160},{160,128},{192,224},{224,1... | collective-permute-start | bytes 1376264 | tf_op jit(solution)/shard_map/ppermute | solution.py:181

commit v9 on v8

--- a/solution.py
+++ b/solution.py
@@ -15,7 +15,8 @@
     return (x % X) * Y + y % Y
 
 
-ORDER = (0, 2, 4, 6, 1, 3, 5, 7)
+ORDER = (0, 7, 1, 6, 2, 5, 3, 4)
+PLACES = [[ORDER.index(4 * h + 2 * k + b) for b in range(2) for h in range(2)] for k in range(2)]
 CLASS_GROUPS = [[tr_of(c - 2 * y, y) for y in ORDER] for c in range(CLASSES)]
 
 FOLD = (0, 7, 1, 6, 2, 5, 3, 4)
@@ -64,21 +65,22 @@
         for block in range(8):
             start = (8 * d + block) * rows
             values = product[start : start + rows]
-            span = pl.ds(block // 2 * rows, rows)
+            owner = 0 if block in PLACES[0] else 1
+            span = pl.ds(PLACES[owner].index(block) * rows, rows)
 
-            @pl.when(core == block % 2)
+            @pl.when(core == owner)
             def _():
                 ours_ref[d, span] = values
 
-            @pl.when(core != block % 2)
+            @pl.when(core != owner)
             def _():
                 theirs_ref[d, span] = values
 
 
 def far_product(side, left_ref, up_ref, integrals_ref, out_ref):
     core = lax.rem(this_core() + side, 2)
-    blocks = [left_ref[core + 2 * i] for i in range(4)]
-    blocks += [up_ref[core + 2 * i] for i in range(4)]
+    places = [first + core * (second - first) for first, second in zip(*PLACES)]
+    blocks = [ref[place] for ref in (left_ref, up_ref) for place in places]
     product = multiply(blocks, integrals_ref)
     count = out_ref.shape[1]
     out_ref[0] = product[:count]

time: 77.9 us -> 77.3 us (level); the launches traced: 77.3 us -> 75.9 us
  waiting for transfers between devices: 6.02 us -> 2.81 us
  starting transfers between devices: 15.3 us -> 18.5 us
  blocking collectives: 50.4 us -> 49 us
    ppermute x3, waiting for transfers between devices: 5.13 us -> 1.76 us  [exchange(): return lax.ppermute(block, ('grp', 'tr'), pairs)]
    ppermute x1, starting transfers between devices: 4.24 us -> 6.15 us  [on_device(): near_given = lax.ppermute(near_theirs, 'grp', swap)]
    ppermute x3, starting transfers between devices: 8.96 us -> 10.4 us  [exchange(): return lax.ppermute(block, ('grp', 'tr'), pairs)]
    all_to_all x1, blocking collectives: 25.4 us -> 24 us  [on_device(): own = lax.all_to_all(copies, 'tr', 0, 0, axis_index_groups=CLASS_GROUPS)]
where the time goes in v9:
time: 77.3 us; the launch traced here: 75.9 us
  blocking collectives  49 us (63%)
  starting transfers between devices  18.5 us (24%)
  Pallas kernels  3.9 us (5%)
  waiting for transfers between devices  2.81 us (4%)
  other arithmetic  0.86 us (1%)
    all_to_all x1, blocking collectives, on_device(): lax.all_to_all(packed, ('grp', 'tr'), 0, 0, axis_index_groups=Z_GROUPS)  25 us
    all_to_all x1, blocking collectives, on_device(): own = lax.all_to_all(copies, 'tr', 0, 0, axis_index_groups=CLASS_GROUPS)  24 us
    ppermute x3, starting transfers between devices, exchange(): return lax.ppermute(block, ('grp', 'tr'), pairs)  10.4 us
    ppermute x1, starting transfers between devices, on_device(): near_given = lax.ppermute(near_theirs, 'grp', swap)  6.15 us
    pallas_call x6, Pallas kernels, run(): pl.pallas_call(kernel, out_shape=shapes, in_specs=[vmem] * len(operands),...  3.9 us
    ppermute x1, starting transfers between devices, on_device(): far_given = lax.ppermute(far_theirs, 'grp', swap)  1.92 us
    ppermute x3, waiting for transfers between devices, exchange(): return lax.ppermute(block, ('grp', 'tr'), pairs)  1.76 us
  transfers between devices with their start and end apart: 5, of which 2 were waited for; matrix products, arithmetic and copies ran while one was open for 0% of the time, Pallas kernels for 4%

profile of v9, /device:TPU:1, one launch (start us, length us, event | category | flops | bytes accessed | tf_op | source)
XLA Modules:
  0.0 75.9 jit_solution(12259986366115922667)
XLA Ops:
  0.7 0.9 %bitcast_select_fusion = bf16[16,2048]{1,0:T(8,128)(2,1)S(1)} fusion(bf16[16,1,2048]{2,0,1:T(8,128)(2,1)} %param.3, pred[2048]{0:T(1024)(128)(4,1)S(1)} %iota_compare_fusion), kind=kLoop, calls=%fused_computation | loop fusion | flops 32768 | bytes 133120 | tf_op jit(solution)/shard_map/jit(_where)/select_n | solution.py:168
  1.6 24.0 %all_to_all.10.own_ref = bf16[8,16,2048]{2,1,0:T(8,128)(2,1)S(1)} all-to-all(bf16[8,16,2048]{2,1,0:T(8,128)(2,1)S(1)} %broadcast_in_dim.14), channel_id=1, replica_groups={{0,23,17,6,2,21,19,4},{8,31,25,14,10,29,27,12},{16,7,1,22,18,5,3,20},{2..., dimensions={0} | all-to-all | bytes 1048576 | tf_op jit(solution)/shard_map/all_to_all | solution.py:170
  25.6 0.0 copy-start
  25.6 2.2 %collective-permute-start = (bf16[8,16,2048]{2,1,0:T(8,128)(2,1)S(1)}, bf16[8,16,2048]{2,1,0:T(8,128)(2,1)S(1)}, u32[]{:S(2)}, u32[]{:S(2)}) collective-permute-start(bf16[8,16,2048]{2,1,0:T(8,128)(2,1)S(1)} %all_to_all.10.own_ref), channel_id=1, source_target_pairs={{8,0},{9,1},{10,2},{11,3},{12,4},{13,5},{14,6},{15,7},{0,8},{1,9},... | collective-permute-start | bytes 1572872 | tf_op jit(solution)/shard_map/ppermute | solution.py:44
  27.8 3.0 %collective-permute-start.2 = (bf16[8,16,2048]{2,1,0:T(8,128)(2,1)S(1)}, bf16[8,16,2048]{2,1,0:T(8,128)(2,1)S(1)}, u32[]{:S(2)}, u32[]{:S(2)}) collective-permute-start(bf16[8,16,2048]{2,1,0:T(8,128)(2,1)S(1)} %all_to_all.10.own_ref), channel_id=1, source_target_pairs={{24,0},{25,1},{26,2},{27,3},{28,4},{29,5},{30,6},{31,7},{16,8},{17... | collective-permute-start | bytes 1572872 | tf_op jit(solution)/shard_map/ppermute | solution.py:44
  30.8 5.2 %collective-permute-start.3 = (bf16[8,16,2048]{2,1,0:T(8,128)(2,1)S(1)}, bf16[8,16,2048]{2,1,0:T(8,128)(2,1)S(1)}, u32[]{:S(2)}, u32[]{:S(2)}) collective-permute-start(bf16[8,16,2048]{2,1,0:T(8,128)(2,1)S(1)} %copy_own.1), channel_id=1, source_target_pairs={{1,0},{0,1},{3,2},{2,3},{5,4},{4,5},{7,6},{6,7},{9,8},{8,9},{11,10... | collective-permute-start | bytes 1572872 | tf_op jit(solution)/shard_map/ppermute | solution.py:44
  36.1 1.8 %collective-permute-done.right_ref = bf16[8,16,2048]{2,1,0:T(8,128)(2,1)S(1)} collective-permute-done((bf16[8,16,2048]{2,1,0:T(8,128)(2,1)S(1)}, bf16[8,16,2048]{2,1,0:T(8,128)(2,1)S(1)}, u32[]{:S(2)}, u32[]{:S(2)}) %collective-permute-start) | collective-permute-done | bytes 524320 | tf_op jit(solution)/shard_map/ppermute | solution.py:44
  37.8 0.0 copy-done
  37.8 1.4 %near.1 = (f32[2,64,896]{2,1,0:T(8,128)S(1)}, f32[2,64,896]{2,1,0:T(8,128)S(1)}) custom-call(bf16[8,16,2048]{2,1,0:T(8,128)(2,1)S(1)} %all_to_all.10.own_ref, bf16[8,16,2048]{2,1,0:T(8,128)(2,1)S(1)} %collective-permute-done.right_ref, bf16[1,2048,896]{2,1,0:T(8,128)(2,1)S(1)} %copy-done), custom_call_target="tpu_custom_call" | custom-call | flops 939524096 | bytes 5636096 | tf_op jit(solution)/shard_map/near/pallas_call | solution.py:151
  39.2 6.1 %collective-permute-start.1 = (f32[2,64,896]{2,1,0:T(8,128)S(1)}, f32[2,64,896]{2,1,0:T(8,128)S(1)}, u32[]{:S(2)}, u32[]{:S(2)}) collective-permute-start(f32[2,64,896]{2,1,0:T(8,128)S(1)} %get-tuple-element.8), channel_id=1, source_target_pairs={{0,32},{32,0},{64,96},{96,64},{128,160},{160,128},{192,224},{224,1... | collective-permute-start | bytes 1376264 | tf_op jit(solution)/shard_map/ppermute | solution.py:181
  45.4 0.0 collective-permute-done.2.left_ref
  45.4 0.0 collective-permute-done.3.up_ref
  45.4 0.7 far_theirs.1
  46.1 1.9 %collective-permute-start.4 = (f32[2,64,896]{2,1,0:T(8,128)S(1)}, f32[2,64,896]{2,1,0:T(8,128)S(1)}, u32[]{:S(2)}, u32[]{:S(2)}) collective-permute-start(f32[2,64,896]{2,1,0:T(8,128)S(1)} %far_theirs.1), channel_id=1, source_target_pairs={{0,32},{32,0},{64,96},{96,64},{128,160},{160,128},{192,224},{224,1... | collective-permute-start | bytes 1376264 | tf_op jit(solution)/shard_map/ppermute | solution.py:183
  48.0 0.7 far_ours.1.far_ours_ref
  48.8 0.0 collective-permute-done.1.near_given_ref
  48.8 1.0 %collective-permute-done.4.far_given_ref = f32[2,64,896]{2,1,0:T(8,128)S(1)} collective-permute-done((f32[2,64,896]{2,1,0:T(8,128)S(1)}, f32[2,64,896]{2,1,0:T(8,128)S(1)}, u32[]{:S(2)}, u32[]{:S(2)}) %collective-permute-start.4) | collective-permute-done | bytes 458784 | tf_op jit(solution)/shard_map/ppermute | solution.py:183
  49.8 0.3 pack.1
  50.1 25.0 %all_to_all.11.in_ref = s16[8,240,128]{2,1,0:T(8,128)(2,1)S(1)} all-to-all(s16[8,240,128]{2,1,0:T(8,128)(2,1)S(1)} %pack.1), channel_id=1, replica_groups={{0,448,64,384,128,320,192,256},{257,193,321,129,385,65,449,1},{2,450,66..., dimensions={0} | all-to-all | bytes 983040 | tf_op jit(solution)/shard_map/all_to_all | solution.py:187
  75.1 0.8 %unpack_sum.1 = bf16[32,896]{1,0:T(8,128)(2,1)} custom-call(s16[8,240,128]{2,1,0:T(8,128)(2,1)S(1)} %all_to_all.11.in_ref), custom_call_target="tpu_custom_call" | custom-call | bytes 548864 | tf_op jit(solution)/shard_map/unpack_sum/pallas_call | solution.py:151
  (3 shorter events, 0.1 us)
Async XLA Ops:
  25.6 12.2 %copy-start = (bf16[1,2048,896]{2,1,0:T(8,128)(2,1)S(1)}, bf16[1,2048,896]{2,1,0:T(8,128)(2,1)}, u32[]{:S(2)}) copy-start(bf16[1,2048,896]{2,1,0:T(8,128)(2,1)} %integrals_ref.5) | copy-start | bytes 11010052
  25.6 12.2 %collective-permute-start = (bf16[8,16,2048]{2,1,0:T(8,128)(2,1)S(1)}, bf16[8,16,2048]{2,1,0:T(8,128)(2,1)S(1)}, u32[]{:S(2)}, u32[]{:S(2)}) collective-permute-start(bf16[8,16,2048]{2,1,0:T(8,128)(2,1)S(1)} %all_to_all.10.own_ref), channel_id=1, source_target_pairs={{8,0},{9,1},{10,2},{11,3},{12,4},{13,5},{14,6},{15,7},{0,8},{1,9},... | collective-permute-start | bytes 1572872 | tf_op jit(solution)/shard_map/ppermute | solution.py:44
  27.8 17.6 %collective-permute-start.2 = (bf16[8,16,2048]{2,1,0:T(8,128)(2,1)S(1)}, bf16[8,16,2048]{2,1,0:T(8,128)(2,1)S(1)}, u32[]{:S(2)}, u32[]{:S(2)}) collective-permute-start(bf16[8,16,2048]{2,1,0:T(8,128)(2,1)S(1)} %all_to_all.10.own_ref), channel_id=1, source_target_pairs={{24,0},{25,1},{26,2},{27,3},{28,4},{29,5},{30,6},{31,7},{16,8},{17... | collective-permute-start | bytes 1572872 | tf_op jit(solution)/shard_map/ppermute | solution.py:44
  30.8 14.6 %collective-permute-start.3 = (bf16[8,16,2048]{2,1,0:T(8,128)(2,1)S(1)}, bf16[8,16,2048]{2,1,0:T(8,128)(2,1)S(1)}, u32[]{:S(2)}, u32[]{:S(2)}) collective-permute-start(bf16[8,16,2048]{2,1,0:T(8,128)(2,1)S(1)} %copy_own.1), channel_id=1, source_target_pairs={{1,0},{0,1},{3,2},{2,3},{5,4},{4,5},{7,6},{6,7},{9,8},{8,9},{11,10... | collective-permute-start | bytes 1572872 | tf_op jit(solution)/shard_map/ppermute | solution.py:44
  39.2 9.6 %collective-permute-start.1 = (f32[2,64,896]{2,1,0:T(8,128)S(1)}, f32[2,64,896]{2,1,0:T(8,128)S(1)}, u32[]{:S(2)}, u32[]{:S(2)}) collective-permute-start(f32[2,64,896]{2,1,0:T(8,128)S(1)} %get-tuple-element.8), channel_id=1, source_target_pairs={{0,32},{32,0},{64,96},{96,64},{128,160},{160,128},{192,224},{224,1... | collective-permute-start | bytes 1376264 | tf_op jit(solution)/shard_map/ppermute | solution.py:181
  46.1 3.7 %collective-permute-start.4 = (f32[2,64,896]{2,1,0:T(8,128)S(1)}, f32[2,64,896]{2,1,0:T(8,128)S(1)}, u32[]{:S(2)}, u32[]{:S(2)}) collective-permute-start(f32[2,64,896]{2,1,0:T(8,128)S(1)} %far_theirs.1), channel_id=1, source_target_pairs={{0,32},{32,0},{64,96},{96,64},{128,160},{160,128},{192,224},{224,1... | collective-permute-start | bytes 1376264 | tf_op jit(solution)/shard_map/ppermute | solution.py:183
